TPU v7x, 32 devices: a whole 2x2x4 slice. The times are simulated.
32 devices in a mesh: section: 16 (over z, x, core), row: 2 (over y).
Axes of the slice: x: 2, y: 2, z: 4, core: 2. Of those that a mesh axis runs over, the one named last changes fastest.
Arguments:
- fwd_queue: bfloat16 [16, 3, 8, 32, 320], P('section', None, 'row'), may hold values from -45 to 45
- bwd_queue: bfloat16 [16, 3, 8, 32, 320], P('section', None, 'row'), may hold values from -6 to 6
- mirror_queue: bfloat16 [16, 3, 8, 32, 320], P('section', None, 'row'), may hold values from -45 to 45
- stash: bfloat16 [16, 3, 2, 8, 32, 320], P('section', None, None, 'row'), may hold values from -45 to 45
- weights: bfloat16 [16, 2, 3, 3, 320, 320], P('section', None, None, None, 'row'), may hold values from -0.109375 to 0.109375
- grad_acc: float32 [16, 2, 3, 3, 320, 320], P('section', None, None, None, 'row'), may hold values from -6 to 6
- fwd_slot: int32 [16, 2], replicated, may hold values from 0 to 2
- bwd_slot: int32 [16, 2], replicated, may hold values from 0 to 2
Outputs:
- forward_queue_after: bfloat16 [16, 3, 8, 32, 320], P('section', None, 'row')
- next_grads: bfloat16 [16, 3, 8, 32, 320], P('section', None, 'row')
- next_mirror: bfloat16 [16, 3, 8, 32, 320], P('section', None, 'row')
- next_stash: bfloat16 [16, 3, 2, 8, 32, 320], P('section', None, None, 'row')
- grad_total: float32 [16, 2, 3, 3, 320, 320], P('section', None, None, None, 'row')
- section_outputs: bfloat16 [16, 2, 8, 32, 320], P('section', None, 'row')
All inputs are finite; a program needn't handle non-finite values.
Results may differ from a plain program's by a relative error of at most 0.012.
Values may be sent and summed in bfloat16 or wider, within the bound.
No kernel may reach another device: no remote copies, remote signals or barrier semaphores. Data moves between devices by JAX's collectives and lax.ppermute only.
A program may use at most 128 MiB of HBM per device.

v0:
```python
import jax
import jax.numpy as jnp
from jax import lax
from jax.sharding import PartitionSpec as P

GROUPS = 32
TICKS = 2


epsilon = 1e-05


def extended(array, sides, width):
    for axis, dim in sides:
        devices, length = (lax.axis_size(axis), array.shape[dim])
        up = [(i, (i + 1) % devices) for i in range(devices - 1)]
        down = [(j, i) for i, j in up]
        last = lax.slice_in_dim(array, length - width, length, axis=dim)
        initial = lax.slice_in_dim(array, 0, width, axis=dim)
        before = lax.ppermute(last, axis, up)
        after = lax.ppermute(initial, axis, down)
        array = jnp.concatenate([before, array, after], axis=dim)
    return array


def partner_2(block, axis, bit):
    count = lax.axis_size(axis)
    route = []
    for low in range(count):
        high = low | 1 << bit
        if high != low and high < count:
            route += [(low, high), (high, low)]
    return lax.ppermute(block, axis, route)


def from_behind(value, axis, steps):
    count = lax.axis_size(axis)
    initial, last = (max(0, -steps), min(count, count - steps))
    return lax.ppermute(value, axis, [(source, source + steps) for source in range(initial, last)])


def patches(padded, row_tally, col_count):
    widened = jnp.pad(padded, ((0, 0), (1, 1), (0, 0)))
    pieces = [
        widened[row_offset : row_offset + row_tally, column_offset : column_offset + col_count, :]
        for row_offset in range(3)
        for column_offset in range(3)
    ]
    return jnp.concatenate(pieces, axis=2).reshape(row_tally * col_count, -1)


def with_rims(tensor):
    return extended(tensor, (("row", 0),), 1)


def input_rims(tensor):
    return extended(tensor, (("row", 0),), 1)


def convolve_padded(padded, kernel):
    row_tally, col_count = (padded.shape[0] - 2, padded.shape[1])
    result = jnp.dot(
        patches(padded, row_tally, col_count),
        kernel.reshape(-1, kernel.shape[-1]),
        preferred_element_type=jnp.float32,
    )
    return result.reshape(row_tally, col_count, -1)


def flipped(kernel):
    return jnp.transpose(kernel[::-1, ::-1], (0, 1, 3, 2))


def grouped(tensor):
    return tensor.astype(jnp.float32).reshape(-1, GROUPS, tensor.shape[-1] // GROUPS)


def apply_norm(tensor, total_sum, total_square, number):
    values = grouped(tensor)
    center = total_sum / number
    spread = total_square / number - center * center
    factor = lax.rsqrt(spread + epsilon)
    return ((values - center[None, :, None]) * factor[None, :, None], factor)


def forward_norm(tensor, number):
    values = grouped(tensor)
    total_sum, total_square = lax.psum(
        (jnp.sum(values, axis=(0, 2)), jnp.sum(values * values, axis=(0, 2))), "row"
    )
    return apply_norm(tensor, total_sum, total_square, number)


def stash_norms(first_tensor, second_tensor, number):
    first_values = grouped(first_tensor)
    second_values = grouped(second_tensor)
    first_sum, first_square, second_sum, second_square = lax.psum(
        (
            jnp.sum(first_values, axis=(0, 2)),
            jnp.sum(first_values * first_values, axis=(0, 2)),
            jnp.sum(second_values, axis=(0, 2)),
            jnp.sum(second_values * second_values, axis=(0, 2)),
        ),
        "row",
    )
    return (
        apply_norm(first_tensor, first_sum, first_square, number),
        apply_norm(second_tensor, second_sum, second_square, number),
    )


def activate(normed, target_shape):
    return jax.nn.silu(normed).reshape(target_shape).astype(jnp.bfloat16)


def norm_back(normed, factor, upstream, number):
    upstream = upstream.reshape(normed.shape)
    logistic = jax.nn.sigmoid(normed)
    gated_grad = upstream * logistic * (1.0 + normed * (1.0 - logistic))
    first_total, second_total = lax.psum(
        (jnp.sum(gated_grad, axis=(0, 2)), jnp.sum(gated_grad * normed, axis=(0, 2))), "row"
    )
    first_mean = first_total / number
    second_mean = second_total / number
    return factor[None, :, None] * (
        gated_grad - first_mean[None, :, None] - normed * second_mean[None, :, None]
    )


def mirror(payload):
    section_tally = lax.axis_size("section")
    bit_count = section_tally.bit_length() - 1
    for bit_number in range(bit_count - 1, -1, -1):
        payload = partner_2(payload, "section", bit_number)
    return payload


def read_slot(queue, slot_index):
    return lax.dynamic_index_in_dim(queue, slot_index, 0, keepdims=False)


def write_slot(queue, slot_index, value_block):
    return lax.dynamic_update_index_in_dim(queue, value_block, slot_index, 0)


def per_device(fwd_queue, bwd_queue, mirror_queue, stash, weights, grad_acc, fwd_slot, bwd_slot):
    section_tally = lax.axis_size("section")
    row_devices = lax.axis_size("row")
    section_index = lax.axis_index("section")
    encoder = section_index < section_tally // 2
    prior_section = jnp.maximum(section_index - 1, 0)
    later_section = jnp.minimum(section_index + 1, section_tally - 1)
    partner = section_tally - 1 - section_index
    inputs_now, grads_now, mirror_now, stash_now = (
        fwd_queue[0],
        bwd_queue[0],
        mirror_queue[0],
        stash[0],
    )
    rows_local, col_count, channels = (
        inputs_now.shape[1],
        inputs_now.shape[2],
        inputs_now.shape[3],
    )
    number = rows_local * row_devices * col_count * (channels // GROUPS)
    kernels = lax.all_gather(weights[0], "row", axis=3, tiled=True)
    first_kernel, second_kernel = (kernels[0], kernels[1])
    first_back, second_back = (flipped(first_kernel), flipped(second_kernel))
    first_inputs, first_outputs, second_inputs, second_outputs = ([], [], [], [])
    emitted = []
    for tick_index in range(TICKS):
        fwd_here = fwd_slot[section_index, tick_index]
        bwd_here = bwd_slot[section_index, tick_index]
        inputs_fwd = read_slot(inputs_now, fwd_here)
        target_shape = inputs_fwd.shape
        skip_fwd = read_slot(mirror_now, fwd_here)
        normed, factor = forward_norm(inputs_fwd, number)
        conv_first = convolve_padded(with_rims(activate(normed, target_shape)), first_kernel)
        second_in = jnp.where(encoder, conv_first.astype(jnp.bfloat16), skip_fwd)
        normed, factor = forward_norm(second_in, number)
        conv_second = convolve_padded(with_rims(activate(normed, target_shape)), second_kernel)
        output = (
            inputs_fwd.astype(jnp.float32) + conv_second + jnp.where(encoder, 0.0, conv_first)
        ).astype(jnp.bfloat16)
        grads_bwd = read_slot(grads_now, bwd_here)
        skip_bwd = read_slot(mirror_now, bwd_here)
        out_grad = (
            grads_bwd.astype(jnp.float32) + jnp.where(encoder, skip_bwd.astype(jnp.float32), 0.0)
        ).astype(jnp.bfloat16)
        stash_pair = read_slot(stash_now, bwd_here)
        (normed_h, factor_h), (normed_i, factor_i) = stash_norms(
            stash_pair[0], stash_pair[1], number
        )
        redo_first = activate(normed_h, target_shape)
        redo_second = activate(normed_i, target_shape)
        back_second = convolve_padded(with_rims(out_grad), second_back)
        skip_grad = (
            norm_back(normed_i, factor_i, back_second, number)
            .reshape(target_shape)
            .astype(jnp.bfloat16)
        )
        first_grad = jnp.where(encoder, skip_grad, out_grad)
        back_first = convolve_padded(with_rims(first_grad), first_back)
        input_grad = (
            out_grad.astype(jnp.float32)
            + norm_back(normed_h, factor_h, back_first, number).reshape(target_shape)
        ).astype(jnp.bfloat16)
        first_inputs.append(patches(input_rims(redo_first), rows_local, col_count))
        first_outputs.append(first_grad.reshape(-1, channels))
        second_inputs.append(patches(input_rims(redo_second), rows_local, col_count))
        second_outputs.append(out_grad.reshape(-1, channels))
        arrived = from_behind(output, "section", 1)
        returned = from_behind(input_grad, "section", -1)
        mirrored = mirror(jnp.where(encoder, output, skip_grad))
        arrive_slot = fwd_slot[prior_section, tick_index]
        inputs_now = write_slot(
            inputs_now,
            arrive_slot,
            jnp.where(section_index > 0, arrived, read_slot(inputs_now, arrive_slot)),
        )
        return_slot = bwd_slot[later_section, tick_index]
        grads_now = write_slot(
            grads_now,
            return_slot,
            jnp.where(
                section_index < section_tally - 1, returned, read_slot(grads_now, return_slot)
            ),
        )
        mirror_slot = jnp.where(
            encoder, bwd_slot[partner, tick_index], fwd_slot[partner, tick_index]
        )
        mirror_now = write_slot(mirror_now, mirror_slot, mirrored)
        stash_now = write_slot(stash_now, fwd_here, jnp.stack([inputs_fwd, second_in]))
        emitted.append(output)
    first_term = jnp.einsum(
        "pk,pd->kd",
        jnp.concatenate(first_inputs, axis=0),
        jnp.concatenate(first_outputs, axis=0),
        preferred_element_type=jnp.float32,
    )
    second_term = jnp.einsum(
        "pk,pd->kd",
        jnp.concatenate(second_inputs, axis=0),
        jnp.concatenate(second_outputs, axis=0),
        preferred_element_type=jnp.float32,
    )
    local_total = jnp.stack([first_term, second_term])
    shared = lax.psum_scatter(
        local_total.reshape(2, 3, 3, channels, channels).astype(jnp.bfloat16),
        "row",
        scatter_dimension=3,
        tiled=True,
    ).astype(jnp.float32)
    grad_total = grad_acc[0] + shared
    return (
        inputs_now[None],
        grads_now[None],
        mirror_now[None],
        stash_now[None],
        grad_total[None],
        jnp.stack(emitted)[None],
    )


def solution(mesh):
    return jax.shard_map(
        per_device,
        mesh=mesh,
        in_specs=(
            P("section", None, "row", None, None),
            P("section", None, "row", None, None),
            P("section", None, "row", None, None),
            P("section", None, None, "row", None, None),
            P("section", None, None, None, "row", None),
            P("section", None, None, None, "row", None),
            P(),
            P(),
        ),
        out_specs=(
            P("section", None, "row", None, None),
            P("section", None, "row", None, None),
            P("section", None, "row", None, None),
            P("section", None, None, "row", None, None),
            P("section", None, None, None, "row", None),
            P("section", None, "row", None, None),
        ),
        check_vma=False,
    )
```

profile of v0, /device:TPU:0, one launch (start us, length us, event | category | flops | bytes accessed | tf_op | source)
XLA Modules:
  0.0 405.0 jit_solution(15951750724742290215)
XLA Ops:
  13.8 4.9 %collective-permute-start.7 = (bf16[1,32,320]{2,1,0:T(8,128)(2,1)S(1)}, bf16[1,32,320]{2,1,0:T(8,128)(2,1)S(1)}, u32[]{:S(2)}, u32[]{:S(2)}) collective-permute-start(bf16[1,32,320]{2,1,0:T(8,128)(2,1)S(1)} %get-tuple-element.187), channel_id=1, source_target_pairs={{0,1},{2,3},{4,5},{6,7},{8,9},{10,11},{12,13},{14,15},{16,17},{18,... | collective-permute-start | bytes 61448 | tf_op jit(solution)/shard_map/ppermute | solution.py:20
  22.5 5.6 %all-reduce.16 = (f32[32]{0:T(128)S(1)}, f32[32]{0:T(128)S(1)}) all-reduce(f32[32]{0:T(128)S(1)} %reduce_sum.289, f32[32]{0:T(128)S(1)} %reduce_sum.295), channel_id=1, replica_groups=mesh['section'=16,'row'=2] {'row'}, use_global_device_ids=true, to_apply=%region_20.21 | all-reduce | flops 64 | bytes 512 | tf_op jit(solution)/shard_map/psum | solution.py:97
  47.0 25.4 %all-gather.3.cloned.1.call-done = bf16[1,2,3,3,320,320]{5,4,3,2,1,0:T(8,128)(2,1)} async-done(((bf16[1,2,3,3,160,320]{5,4,3,2,1,0:T(8,128)(2,1)}), bf16[1,2,3,3,320,320]{5,4,3,2,1,0:T(8,128)(2,1)}) %all-gather.3.cloned.1.call-update) | async-done | bytes 3686416 | tf_op jit(solution)/shard_map/all_gather | solution.py:166
  72.4 5.1 %fusion.81 = (bf16[1,1,3,3,320,320]{5,4,3,2,1,0:T(8,128)(2,1)}, bf16[3,3,320,320]{3,2,1,0:T(8,128)(2,1)S(1)}, bf16[3,3,320,320]{3,2,1,0:T(8,128)(2,1)S(1)}, bf16[1,1,3,3,320,320]{5,4,3,2,1,0:T(8,128)(2,1)S(1)}) fusion(bf16[1,2,3,3,320,320]{5,4,3,2,1,0:T(8,128)(2,1)} %all-gather.3.cloned.1.call-done), kind=kLoop, calls=%fused_computation.254 | loop fusion | bytes 11059200 | tf_op jit(solution)/shard_map/slice | solution.py:167
  77.5 2.5 reverse_bitcast_fusion
  80.0 4.2 %copy.33 = bf16[3,3,320,320]{3,2,1,0:T(8,128)(2,1)} copy(bf16[3,3,320,320]{2,3,1,0:T(8,128)(2,1)} %get-tuple-element.234) | data formatting | bytes 3686400 | tf_op jit(solution)/shard_map/transpose | solution.py:71
  84.2 4.0 copy.34
  88.3 4.2 %dot_general.42 = bf16[32,10,2880]{2,1,0:T(8,128)(2,1)} reshape(bf16[320,2880]{1,0:T(8,128)(2,1)} %copy.34) | data formatting | bytes 3686400 | tf_op jit(solution)/shard_map/dot_general | solution.py:62
  92.5 3.6 fusion.80
  96.1 5.5 %all-reduce.15 = (f32[32]{0:T(128)}, f32[32]{0:T(128)}, f32[32]{0:T(128)S(1)}, f32[32]{0:T(128)S(1)}, f32[32]{0:T(128)}, /*index=5*/f32[32]{0:T(128)}) all-reduce(f32[32]{0:T(128)S(1)} %copy-done.27, f32[32]{0:T(128)S(1)} %copy-done.26, f32[32]{0:T(128)S(1)} %get-tuple-element.23, ...), channel_id=1, replica_groups=mesh['section'=16,'row'=2] {'row'}, use_global_device_ids=true, to_apply=%region_5.6 | all-reduce | flops 192 | bytes 1536 | tf_op jit(solution)/shard_map/psum | solution.py:88
  106.1 2.2 collective-permute-start.16
  113.3 5.1 %collective-permute-start = (bf16[1,32,320]{2,1,0:T(8,128)(2,1)}, bf16[1,32,320]{2,1,0:T(8,128)(2,1)}, u32[]{:S(2)}, u32[]{:S(2)}) collective-permute-start(bf16[1,32,320]{2,1,0:T(8,128)(2,1)} %get-tuple-element.183), channel_id=1, source_target_pairs={{0,1},{2,3},{4,5},{6,7},{8,9},{10,11},{12,13},{14,15},{16,17},{18,... | collective-permute-start | bytes 61448 | tf_op jit(solution)/shard_map/ppermute | solution.py:20
  121.2 5.7 %collective-permute-start.28 = (bf16[1,32,320]{2,1,0:T(8,128)(2,1)}, bf16[1,32,320]{2,1,0:T(8,128)(2,1)}, u32[]{:S(2)}, u32[]{:S(2)}) collective-permute-start(bf16[1,32,320]{2,1,0:T(8,128)(2,1)} %get-tuple-element.143), channel_id=1, source_target_pairs={{0,1},{2,3},{4,5},{6,7},{8,9},{10,11},{12,13},{14,15},{16,17},{18,... | collective-permute-start | bytes 61448 | tf_op jit(solution)/shard_map/ppermute | solution.py:20
  129.1 4.3 %copy.43 = bf16[3,3,320,320]{3,2,1,0:T(8,128)(2,1)} copy(bf16[3,3,320,320]{2,3,1,0:T(8,128)(2,1)} %get-tuple-element.233) | data formatting | bytes 3686400 | tf_op jit(solution)/shard_map/transpose | solution.py:71
  133.4 4.1 %copy.44 = bf16[320,2880]{1,0:T(8,128)(2,1)} copy(bf16[320,2880]{0,1:T(8,128)(2,1)} %bitcast.239) | data formatting | bytes 3686400 | tf_op jit(solution)/shard_map/dot_general | solution.py:62
  137.5 4.2 %dot_general.46 = bf16[32,10,2880]{2,1,0:T(8,128)(2,1)} reshape(bf16[320,2880]{1,0:T(8,128)(2,1)} %copy.44) | data formatting | bytes 3686400 | tf_op jit(solution)/shard_map/dot_general | solution.py:62
  143.1 5.7 %collective-permute-start.32 = (bf16[1,32,320]{2,1,0:T(8,128)(2,1)}, bf16[1,32,320]{2,1,0:T(8,128)(2,1)}, u32[]{:S(2)}, u32[]{:S(2)}) collective-permute-start(bf16[1,32,320]{2,1,0:T(8,128)(2,1)} %get-tuple-element.151), channel_id=1, source_target_pairs={{0,1},{2,3},{4,5},{6,7},{8,9},{10,11},{12,13},{14,15},{16,17},{18,... | collective-permute-start | bytes 61448 | tf_op jit(solution)/shard_map/ppermute | solution.py:20
  156.5 3.0 convert_reduce_fusion.3
  169.4 3.5 fusion.79
  172.9 6.8 %all-reduce.14 = (f32[32]{0:T(128)}, f32[32]{0:T(128)}, f32[32]{0:T(128)}, f32[32]{0:T(128)}, f32[32]{0:T(128)}, /*index=5*/f32[32]{0:T(128)}) all-reduce(f32[32]{0:T(128)} %reduce_sum.274, f32[32]{0:T(128)} %reduce_sum.268, f32[32]{0:T(128)} %get-tuple-element.21, ...), channel_id=1, replica_groups=mesh['section'=16,'row'=2] {'row'}, use_global_device_ids=true, to_apply=%region_11.12 | all-reduce | flops 192 | bytes 1536 | tf_op jit(solution)/shard_map/psum | solution.py:88
  192.1 3.9 collective-permute-start.2
  215.6 3.1 broadcast_select_fusion.3
  218.7 3.3 collective-permute-start.9
  241.8 4.3 %collective-permute-start.19 = (bf16[1,32,320]{2,1,0:T(8,128)(2,1)S(1)}, bf16[1,32,320]{2,1,0:T(8,128)(2,1)S(1)}, u32[]{:S(2)}, u32[]{:S(2)}) collective-permute-start(bf16[1,32,320]{2,1,0:T(8,128)(2,1)S(1)} %get-tuple-element.171), channel_id=1, source_target_pairs={{0,1},{2,3},{4,5},{6,7},{8,9},{10,11},{12,13},{14,15},{16,17},{18,... | collective-permute-start | bytes 61448 | tf_op jit(solution)/shard_map/ppermute | solution.py:20
  255.5 3.4 fusion.78
  258.9 5.6 %all-reduce.13 = (f32[32]{0:T(128)}, f32[32]{0:T(128)}, f32[32]{0:T(128)}, f32[32]{0:T(128)}, f32[32]{0:T(128)}, /*index=5*/f32[32]{0:T(128)}) all-reduce(f32[32]{0:T(128)} %reduce_sum.283, f32[32]{0:T(128)} %reduce_sum.277, f32[32]{0:T(128)} %get-tuple-element.19, ...), channel_id=1, replica_groups=mesh['section'=16,'row'=2] {'row'}, use_global_device_ids=true, to_apply=%region_17.18 | all-reduce | flops 192 | bytes 1536 | tf_op jit(solution)/shard_map/psum | solution.py:88
  269.5 2.5 collective-permute-start.30
  273.9 4.5 %collective-permute-start.34 = (bf16[1,32,320]{2,1,0:T(8,128)(2,1)}, bf16[1,32,320]{2,1,0:T(8,128)(2,1)S(1)}, u32[]{:S(2)}, u32[]{:S(2)}) collective-permute-start(bf16[1,32,320]{2,1,0:T(8,128)(2,1)} %get-tuple-element.155), channel_id=1, source_target_pairs={{0,1},{2,3},{4,5},{6,7},{8,9},{10,11},{12,13},{14,15},{16,17},{18,... | collective-permute-start | bytes 61448 | tf_op jit(solution)/shard_map/ppermute | solution.py:20
  282.9 2.2 concatenate.197
  285.1 3.4 convolution_convert_fusion
  288.4 4.0 copy.68
  296.1 3.3 convolution_convert_fusion.1
  299.5 4.0 copy.69
  303.4 5.2 %pad_maximum_fusion = bf16[2,3,3,320,320]{4,3,2,1,0:T(8,128)(2,1)} fusion(bf16[1,3,3,320,320]{4,3,2,1,0:T(8,128)(2,1)} %bitcast.237, bf16[1,3,3,320,320]{4,3,2,1,0:T(8,128)(2,1)} %bitcast.236), kind=kLoop, calls=%fused_computation | loop fusion | flops 1843200 | bytes 7372800 | tf_op jit(solution)/shard_map/stack | solution.py:247
  315.7 2.2 reshape.292
  323.5 4.5 %collective-permute-start.5 = (bf16[1,32,320]{2,1,0:T(8,128)(2,1)S(1)}, bf16[1,32,320]{2,1,0:T(8,128)(2,1)S(1)}, u32[]{:S(2)}, u32[]{:S(2)}) collective-permute-start(bf16[1,32,320]{2,1,0:T(8,128)(2,1)S(1)} %get-tuple-element.167), channel_id=1, source_target_pairs={{0,1},{2,3},{4,5},{6,7},{8,9},{10,11},{12,13},{14,15},{16,17},{18,... | collective-permute-start | bytes 61448 | tf_op jit(solution)/shard_map/ppermute | solution.py:20
  330.8 4.5 %collective-permute-start.21 = (bf16[1,32,320]{2,1,0:T(8,128)(2,1)}, bf16[1,32,320]{2,1,0:T(8,128)(2,1)S(1)}, u32[]{:S(2)}, u32[]{:S(2)}) collective-permute-start(bf16[1,32,320]{2,1,0:T(8,128)(2,1)} %get-tuple-element.163), channel_id=1, source_target_pairs={{0,1},{2,3},{4,5},{6,7},{8,9},{10,11},{12,13},{14,15},{16,17},{18,... | collective-permute-start | bytes 61448 | tf_op jit(solution)/shard_map/ppermute | solution.py:20
  338.5 2.1 concatenate.169
  340.6 2.4 convert_reduce_fusion.2
  344.2 2.7 fusion.77
  346.9 5.6 %all-reduce.12 = (f32[32]{0:T(128)S(1)}, f32[32]{0:T(128)S(1)}, f32[32]{0:T(128)S(1)}, f32[32]{0:T(128)S(1)}) all-reduce(f32[32]{0:T(128)S(1)} %reduce_sum.359, f32[32]{0:T(128)S(1)} %reduce_sum.356, f32[32]{0:T(128)S(1)} %get-tuple-element.17, f32[32]{0:T(128)S(1)} %get-tuple-element.16), channel_id=1, replica_groups=mesh['section'=16,'row'=2] {'row'}, use_global_device_ids=true, to_apply=%region_33.34 | all-reduce | flops 128 | bytes 1024 | tf_op jit(solution)/shard_map/psum | solution.py:88
  353.6 3.9 collective-permute-start.13
  360.2 2.2 copy.62
  370.8 5.1 %collective-permute-start.24 = (bf16[4,32,320]{2,1,0:T(8,128)(2,1)S(1)}, bf16[4,32,320]{2,1,0:T(8,128)(2,1)S(1)}, u32[]{:S(2)}, u32[]{:S(2)}) collective-permute-start(bf16[4,32,320]{2,1,0:T(8,128)(2,1)S(1)} %get-tuple-element.225), channel_id=1, source_target_pairs={{0,16},{16,0},{2,18},{18,2},{4,20},{20,4},{6,22},{22,6},{8,24},{24... | collective-permute-start | bytes 245768 | tf_op jit(solution)/shard_map/ppermute | solution.py:33
  378.1 3.4 collective-permute-done.24
  382.2 3.9 collective-permute-done.25
  388.2 2.5 collective-permute-done.26
  392.6 5.5 %fusion = f32[1,2,3,3,160,320]{5,4,3,2,1,0:T(8,128)} fusion(f32[1,2,3,3,160,320]{5,4,3,2,1,0:T(8,128)} %param.13, bf16[2,3,3,160,320]{4,3,2,1,0:T(8,128)(2,1)} %reduce-scatter.2.cloned.1.call-done), kind=kLoop, calls=%fused_computation.2 | loop fusion | flops 1843200 | bytes 9216000 | tf_op jit(solution)/shard_map/broadcast_in_dim | solution.py:260
  (330 shorter events, 159.6 us)
Async XLA Ops:
  7.2 65.2 %all-gather.3.cloned.1.call-start = ((), (), s32[]{:S(2)}) async-start(), calls=%async_computation.2 | async-start | bytes 6635520 | tf_op jit(solution)/shard_map/all_gather | solution.py:166
  9.0 19.2 %copy-start.2 = (bf16[1,3,4,32,320]{4,3,2,1,0:T(8,128)(2,1)S(1)}, bf16[1,3,4,32,320]{4,3,2,1,0:T(8,128)(2,1)}, u32[]{:S(2)}) copy-start(bf16[1,3,4,32,320]{4,3,2,1,0:T(8,128)(2,1)} %param.8) | copy-start | bytes 737284
  10.1 382.5 %reduce-scatter.2.cloned.1.call-start = ((), (), s32[]{:S(2)}) async-start(), calls=%async_computation.1 | async-start | bytes 6635520 | tf_op jit(solution)/shard_map/reduce_scatter | solution.py:248
  13.8 31.8 %collective-permute-start.7 = (bf16[1,32,320]{2,1,0:T(8,128)(2,1)S(1)}, bf16[1,32,320]{2,1,0:T(8,128)(2,1)S(1)}, u32[]{:S(2)}, u32[]{:S(2)}) collective-permute-start(bf16[1,32,320]{2,1,0:T(8,128)(2,1)S(1)} %get-tuple-element.187), channel_id=1, source_target_pairs={{0,1},{2,3},{4,5},{6,7},{8,9},{10,11},{12,13},{14,15},{16,17},{18,... | collective-permute-start | bytes 61448 | tf_op jit(solution)/shard_map/ppermute | solution.py:20
  18.7 26.9 %collective-permute-start.8 = (bf16[1,32,320]{2,1,0:T(8,128)(2,1)S(1)}, bf16[1,32,320]{2,1,0:T(8,128)(2,1)S(1)}, u32[]{:S(2)}, u32[]{:S(2)}) collective-permute-start(bf16[1,32,320]{2,1,0:T(8,128)(2,1)S(1)} %get-tuple-element.188), channel_id=1, source_target_pairs={{1,0},{3,2},{5,4},{7,6},{9,8},{11,10},{13,12},{15,14},{17,16},{19,... | collective-permute-start | bytes 61448 | tf_op jit(solution)/shard_map/ppermute | solution.py:21
  28.2 14.2 %copy-start.20 = (f32[32]{0:T(128)}, f32[32]{0:T(128)S(1)}, u32[]{:S(2)}) copy-start(f32[32]{0:T(128)S(1)} %get-tuple-element.215) | copy-start | bytes 388
  28.2 14.2 %copy-start.22 = (f32[32]{0:T(128)}, f32[32]{0:T(128)S(1)}, u32[]{:S(2)}) copy-start(f32[32]{0:T(128)S(1)} %get-tuple-element.216) | copy-start | bytes 388
  106.1 35.6 %collective-permute-start.16 = (bf16[1,32,320]{2,1,0:T(8,128)(2,1)}, bf16[1,32,320]{2,1,0:T(8,128)(2,1)S(1)}, u32[]{:S(2)}, u32[]{:S(2)}) collective-permute-start(bf16[1,32,320]{2,1,0:T(8,128)(2,1)} %get-tuple-element.179), channel_id=1, source_target_pairs={{0,1},{2,3},{4,5},{6,7},{8,9},{10,11},{12,13},{14,15},{16,17},{18,... | collective-permute-start | bytes 61448 | tf_op jit(solution)/shard_map/ppermute | solution.py:20
  108.3 34.8 %collective-permute-start.17 = (bf16[1,32,320]{2,1,0:T(8,128)(2,1)}, bf16[1,32,320]{2,1,0:T(8,128)(2,1)S(1)}, u32[]{:S(2)}, u32[]{:S(2)}) collective-permute-start(bf16[1,32,320]{2,1,0:T(8,128)(2,1)} %get-tuple-element.180), channel_id=1, source_target_pairs={{1,0},{3,2},{5,4},{7,6},{9,8},{11,10},{13,12},{15,14},{17,16},{19,... | collective-permute-start | bytes 61448 | tf_op jit(solution)/shard_map/ppermute | solution.py:21
  113.3 36.4 %collective-permute-start = (bf16[1,32,320]{2,1,0:T(8,128)(2,1)}, bf16[1,32,320]{2,1,0:T(8,128)(2,1)}, u32[]{:S(2)}, u32[]{:S(2)}) collective-permute-start(bf16[1,32,320]{2,1,0:T(8,128)(2,1)} %get-tuple-element.183), channel_id=1, source_target_pairs={{0,1},{2,3},{4,5},{6,7},{8,9},{10,11},{12,13},{14,15},{16,17},{18,... | collective-permute-start | bytes 61448 | tf_op jit(solution)/shard_map/ppermute | solution.py:20
  118.5 32.6 %collective-permute-start.1 = (bf16[1,32,320]{2,1,0:T(8,128)(2,1)}, bf16[1,32,320]{2,1,0:T(8,128)(2,1)}, u32[]{:S(2)}, u32[]{:S(2)}) collective-permute-start(bf16[1,32,320]{2,1,0:T(8,128)(2,1)} %get-tuple-element.184), channel_id=1, source_target_pairs={{1,0},{3,2},{5,4},{7,6},{9,8},{11,10},{13,12},{15,14},{17,16},{19,... | collective-permute-start | bytes 61448 | tf_op jit(solution)/shard_map/ppermute | solution.py:21
  121.2 70.8 %collective-permute-start.28 = (bf16[1,32,320]{2,1,0:T(8,128)(2,1)}, bf16[1,32,320]{2,1,0:T(8,128)(2,1)}, u32[]{:S(2)}, u32[]{:S(2)}) collective-permute-start(bf16[1,32,320]{2,1,0:T(8,128)(2,1)} %get-tuple-element.143), channel_id=1, source_target_pairs={{0,1},{2,3},{4,5},{6,7},{8,9},{10,11},{12,13},{14,15},{16,17},{18,... | collective-permute-start | bytes 61448 | tf_op jit(solution)/shard_map/ppermute | solution.py:20
  141.7 54.4 %collective-permute-start.29 = (bf16[1,32,320]{2,1,0:T(8,128)(2,1)}, bf16[1,32,320]{2,1,0:T(8,128)(2,1)}, u32[]{:S(2)}, u32[]{:S(2)}) collective-permute-start(bf16[1,32,320]{2,1,0:T(8,128)(2,1)} %get-tuple-element.144), channel_id=1, source_target_pairs={{1,0},{3,2},{5,4},{7,6},{9,8},{11,10},{13,12},{15,14},{17,16},{19,... | collective-permute-start | bytes 61448 | tf_op jit(solution)/shard_map/ppermute | solution.py:21
  143.1 55.9 %collective-permute-start.32 = (bf16[1,32,320]{2,1,0:T(8,128)(2,1)}, bf16[1,32,320]{2,1,0:T(8,128)(2,1)}, u32[]{:S(2)}, u32[]{:S(2)}) collective-permute-start(bf16[1,32,320]{2,1,0:T(8,128)(2,1)} %get-tuple-element.151), channel_id=1, source_target_pairs={{0,1},{2,3},{4,5},{6,7},{8,9},{10,11},{12,13},{14,15},{16,17},{18,... | collective-permute-start | bytes 61448 | tf_op jit(solution)/shard_map/ppermute | solution.py:20
  149.8 49.3 %collective-permute-start.33 = (bf16[1,32,320]{2,1,0:T(8,128)(2,1)}, bf16[1,32,320]{2,1,0:T(8,128)(2,1)}, u32[]{:S(2)}, u32[]{:S(2)}) collective-permute-start(bf16[1,32,320]{2,1,0:T(8,128)(2,1)} %get-tuple-element.152), channel_id=1, source_target_pairs={{1,0},{3,2},{5,4},{7,6},{9,8},{11,10},{13,12},{15,14},{17,16},{19,... | collective-permute-start | bytes 61448 | tf_op jit(solution)/shard_map/ppermute | solution.py:21
  185.0 15.7 %copy-start.30 = (f32[32]{0:T(128)S(1)}, f32[32]{0:T(128)}, u32[]{:S(2)}) copy-start(f32[32]{0:T(128)} %get-tuple-element.44) | copy-start | bytes 388
  185.0 15.7 %copy-start.31 = (f32[32]{0:T(128)S(1)}, f32[32]{0:T(128)}, u32[]{:S(2)}) copy-start(f32[32]{0:T(128)} %get-tuple-element.45) | copy-start | bytes 388
  188.6 46.6 %collective-permute-start.18 = (bf16[4,32,320]{2,1,0:T(8,128)(2,1)}, bf16[4,32,320]{2,1,0:T(8,128)(2,1)}, u32[]{:S(2)}, u32[]{:S(2)}) collective-permute-start(bf16[4,32,320]{2,1,0:T(8,128)(2,1)} %add_convert_fusion.2), channel_id=1, source_target_pairs={{2,0},{4,2},{6,4},{8,6},{10,8},{12,10},{14,12},{16,14},{18,16},{20... | collective-permute-start | bytes 245768 | tf_op jit(solution)/shard_map/ppermute | solution.py:39
  192.1 19.8 %collective-permute-start.2 = (bf16[1,32,320]{2,1,0:T(8,128)(2,1)}, bf16[1,32,320]{2,1,0:T(8,128)(2,1)S(1)}, u32[]{:S(2)}, u32[]{:S(2)}) collective-permute-start(bf16[1,32,320]{2,1,0:T(8,128)(2,1)} %get-tuple-element.175), channel_id=1, source_target_pairs={{0,1},{2,3},{4,5},{6,7},{8,9},{10,11},{12,13},{14,15},{16,17},{18,... | collective-permute-start | bytes 61448 | tf_op jit(solution)/shard_map/ppermute | solution.py:20
  196.0 15.8 %collective-permute-start.3 = (bf16[1,32,320]{2,1,0:T(8,128)(2,1)}, bf16[1,32,320]{2,1,0:T(8,128)(2,1)S(1)}, u32[]{:S(2)}, u32[]{:S(2)}) collective-permute-start(bf16[1,32,320]{2,1,0:T(8,128)(2,1)} %get-tuple-element.176), channel_id=1, source_target_pairs={{1,0},{3,2},{5,4},{7,6},{9,8},{11,10},{13,12},{15,14},{17,16},{19,... | collective-permute-start | bytes 61448 | tf_op jit(solution)/shard_map/ppermute | solution.py:21
  218.7 21.4 %copy-start.13 = (bf16[4,32,320]{2,1,0:T(8,128)(2,1)}, bf16[4,32,320]{2,1,0:T(8,128)(2,1)S(1)}, u32[]{:S(2)}) copy-start(bf16[4,32,320]{2,1,0:T(8,128)(2,1)S(1)} %get-tuple-element.221) | copy-start | bytes 245764
  218.7 8.9 %collective-permute-start.9 = (bf16[4,32,320]{2,1,0:T(8,128)(2,1)}, bf16[4,32,320]{2,1,0:T(8,128)(2,1)}, u32[]{:S(2)}, u32[]{:S(2)}) collective-permute-start(bf16[4,32,320]{2,1,0:T(8,128)(2,1)} %get-tuple-element.220), channel_id=1, source_target_pairs={{0,16},{16,0},{2,18},{18,2},{4,20},{20,4},{6,22},{22,6},{8,24},{24... | collective-permute-start | bytes 245768 | tf_op jit(solution)/shard_map/ppermute | solution.py:33
  227.6 5.8 %collective-permute-start.10 = (bf16[4,32,320]{2,1,0:T(8,128)(2,1)}, bf16[4,32,320]{2,1,0:T(8,128)(2,1)}, u32[]{:S(2)}, u32[]{:S(2)}) collective-permute-start(bf16[4,32,320]{2,1,0:T(8,128)(2,1)} %collective-permute-done.9), channel_id=1, source_target_pairs={{0,8},{8,0},{2,10},{10,2},{4,12},{12,4},{6,14},{14,6},{16,24},{24,... | collective-permute-start | bytes 245768 | tf_op jit(solution)/shard_map/ppermute | solution.py:33
  231.8 7.4 %collective-permute-start.4 = (bf16[4,32,320]{2,1,0:T(8,128)(2,1)S(1)}, bf16[4,32,320]{2,1,0:T(8,128)(2,1)S(1)}, u32[]{:S(2)}, u32[]{:S(2)}) collective-permute-start(bf16[4,32,320]{2,1,0:T(8,128)(2,1)S(1)} %get-tuple-element.221), channel_id=1, source_target_pairs={{0,2},{2,4},{4,6},{6,8},{8,10},{10,12},{12,14},{14,16},{16,18},{18... | collective-permute-start | bytes 245768 | tf_op jit(solution)/shard_map/ppermute | solution.py:39
  233.4 5.1 %collective-permute-start.11 = (bf16[4,32,320]{2,1,0:T(8,128)(2,1)}, bf16[4,32,320]{2,1,0:T(8,128)(2,1)S(1)}, u32[]{:S(2)}, u32[]{:S(2)}) collective-permute-start(bf16[4,32,320]{2,1,0:T(8,128)(2,1)} %collective-permute-done.10), channel_id=1, source_target_pairs={{0,4},{4,0},{2,6},{6,2},{8,12},{12,8},{10,14},{14,10},{16,20},{20,... | collective-permute-start | bytes 245768 | tf_op jit(solution)/shard_map/ppermute | solution.py:33
  238.6 1.6 collective-permute-start.12
  241.8 7.9 %collective-permute-start.19 = (bf16[1,32,320]{2,1,0:T(8,128)(2,1)S(1)}, bf16[1,32,320]{2,1,0:T(8,128)(2,1)S(1)}, u32[]{:S(2)}, u32[]{:S(2)}) collective-permute-start(bf16[1,32,320]{2,1,0:T(8,128)(2,1)S(1)} %get-tuple-element.171), channel_id=1, source_target_pairs={{0,1},{2,3},{4,5},{6,7},{8,9},{10,11},{12,13},{14,15},{16,17},{18,... | collective-permute-start | bytes 61448 | tf_op jit(solution)/shard_map/ppermute | solution.py:20
  246.0 5.7 %collective-permute-start.20 = (bf16[1,32,320]{2,1,0:T(8,128)(2,1)S(1)}, bf16[1,32,320]{2,1,0:T(8,128)(2,1)S(1)}, u32[]{:S(2)}, u32[]{:S(2)}) collective-permute-start(bf16[1,32,320]{2,1,0:T(8,128)(2,1)S(1)} %get-tuple-element.172), channel_id=1, source_target_pairs={{1,0},{3,2},{5,4},{7,6},{9,8},{11,10},{13,12},{15,14},{17,16},{19,... | collective-permute-start | bytes 61448 | tf_op jit(solution)/shard_map/ppermute | solution.py:21
  269.5 12.7 %copy-start.5 = (bf16[4,32,320]{2,1,0:T(8,128)(2,1)}, bf16[4,32,320]{2,1,0:T(8,128)(2,1)S(1)}, u32[]{:S(2)}) copy-start(bf16[4,32,320]{2,1,0:T(8,128)(2,1)S(1)} %get-tuple-element.63) | copy-start | bytes 245764
  269.5 11.8 %collective-permute-start.30 = (bf16[1,32,320]{2,1,0:T(8,128)(2,1)S(1)}, bf16[1,32,320]{2,1,0:T(8,128)(2,1)S(1)}, u32[]{:S(2)}, u32[]{:S(2)}) collective-permute-start(bf16[1,32,320]{2,1,0:T(8,128)(2,1)S(1)} %get-tuple-element.147), channel_id=1, source_target_pairs={{0,1},{2,3},{4,5},{6,7},{8,9},{10,11},{12,13},{14,15},{16,17},{18,... | collective-permute-start | bytes 61448 | tf_op jit(solution)/shard_map/ppermute | solution.py:20
  272.0 9.3 %collective-permute-start.31 = (bf16[1,32,320]{2,1,0:T(8,128)(2,1)S(1)}, bf16[1,32,320]{2,1,0:T(8,128)(2,1)S(1)}, u32[]{:S(2)}, u32[]{:S(2)}) collective-permute-start(bf16[1,32,320]{2,1,0:T(8,128)(2,1)S(1)} %get-tuple-element.148), channel_id=1, source_target_pairs={{1,0},{3,2},{5,4},{7,6},{9,8},{11,10},{13,12},{15,14},{17,16},{19,... | collective-permute-start | bytes 61448 | tf_op jit(solution)/shard_map/ppermute | solution.py:21
  273.9 18.5 %collective-permute-start.34 = (bf16[1,32,320]{2,1,0:T(8,128)(2,1)}, bf16[1,32,320]{2,1,0:T(8,128)(2,1)S(1)}, u32[]{:S(2)}, u32[]{:S(2)}) collective-permute-start(bf16[1,32,320]{2,1,0:T(8,128)(2,1)} %get-tuple-element.155), channel_id=1, source_target_pairs={{0,1},{2,3},{4,5},{6,7},{8,9},{10,11},{12,13},{14,15},{16,17},{18,... | collective-permute-start | bytes 61448 | tf_op jit(solution)/shard_map/ppermute | solution.py:20
  278.5 14.0 %collective-permute-start.35 = (bf16[1,32,320]{2,1,0:T(8,128)(2,1)}, bf16[1,32,320]{2,1,0:T(8,128)(2,1)S(1)}, u32[]{:S(2)}, u32[]{:S(2)}) collective-permute-start(bf16[1,32,320]{2,1,0:T(8,128)(2,1)} %get-tuple-element.156), channel_id=1, source_target_pairs={{1,0},{3,2},{5,4},{7,6},{9,8},{11,10},{13,12},{15,14},{17,16},{19,... | collective-permute-start | bytes 61448 | tf_op jit(solution)/shard_map/ppermute | solution.py:21
  308.7 14.3 %copy-start.28 = (f32[32]{0:T(128)S(1)}, f32[32]{0:T(128)}, u32[]{:S(2)}) copy-start(f32[32]{0:T(128)} %get-tuple-element.34) | copy-start | bytes 388
  308.7 14.3 %copy-start.29 = (f32[32]{0:T(128)S(1)}, f32[32]{0:T(128)}, u32[]{:S(2)}) copy-start(f32[32]{0:T(128)} %get-tuple-element.35) | copy-start | bytes 388
  323.5 13.4 %collective-permute-start.5 = (bf16[1,32,320]{2,1,0:T(8,128)(2,1)S(1)}, bf16[1,32,320]{2,1,0:T(8,128)(2,1)S(1)}, u32[]{:S(2)}, u32[]{:S(2)}) collective-permute-start(bf16[1,32,320]{2,1,0:T(8,128)(2,1)S(1)} %get-tuple-element.167), channel_id=1, source_target_pairs={{0,1},{2,3},{4,5},{6,7},{8,9},{10,11},{12,13},{14,15},{16,17},{18,... | collective-permute-start | bytes 61448 | tf_op jit(solution)/shard_map/ppermute | solution.py:20
  328.0 8.9 %collective-permute-start.6 = (bf16[1,32,320]{2,1,0:T(8,128)(2,1)S(1)}, bf16[1,32,320]{2,1,0:T(8,128)(2,1)S(1)}, u32[]{:S(2)}, u32[]{:S(2)}) collective-permute-start(bf16[1,32,320]{2,1,0:T(8,128)(2,1)S(1)} %get-tuple-element.168), channel_id=1, source_target_pairs={{1,0},{3,2},{5,4},{7,6},{9,8},{11,10},{13,12},{15,14},{17,16},{19,... | collective-permute-start | bytes 61448 | tf_op jit(solution)/shard_map/ppermute | solution.py:21
  330.8 12.6 %collective-permute-start.21 = (bf16[1,32,320]{2,1,0:T(8,128)(2,1)}, bf16[1,32,320]{2,1,0:T(8,128)(2,1)S(1)}, u32[]{:S(2)}, u32[]{:S(2)}) collective-permute-start(bf16[1,32,320]{2,1,0:T(8,128)(2,1)} %get-tuple-element.163), channel_id=1, source_target_pairs={{0,1},{2,3},{4,5},{6,7},{8,9},{10,11},{12,13},{14,15},{16,17},{18,... | collective-permute-start | bytes 61448 | tf_op jit(solution)/shard_map/ppermute | solution.py:20
  335.4 8.1 %collective-permute-start.22 = (bf16[1,32,320]{2,1,0:T(8,128)(2,1)}, bf16[1,32,320]{2,1,0:T(8,128)(2,1)S(1)}, u32[]{:S(2)}, u32[]{:S(2)}) collective-permute-start(bf16[1,32,320]{2,1,0:T(8,128)(2,1)} %get-tuple-element.164), channel_id=1, source_target_pairs={{1,0},{3,2},{5,4},{7,6},{9,8},{11,10},{13,12},{15,14},{17,16},{19,... | collective-permute-start | bytes 61448 | tf_op jit(solution)/shard_map/ppermute | solution.py:21
  353.6 11.8 %collective-permute-start.13 = (bf16[1,32,320]{2,1,0:T(8,128)(2,1)}, bf16[1,32,320]{2,1,0:T(8,128)(2,1)S(1)}, u32[]{:S(2)}, u32[]{:S(2)}) collective-permute-start(bf16[1,32,320]{2,1,0:T(8,128)(2,1)} %get-tuple-element.159), channel_id=1, source_target_pairs={{0,1},{2,3},{4,5},{6,7},{8,9},{10,11},{12,13},{14,15},{16,17},{18,... | collective-permute-start | bytes 61448 | tf_op jit(solution)/shard_map/ppermute | solution.py:20
  357.5 7.9 %collective-permute-start.14 = (bf16[1,32,320]{2,1,0:T(8,128)(2,1)}, bf16[1,32,320]{2,1,0:T(8,128)(2,1)S(1)}, u32[]{:S(2)}, u32[]{:S(2)}) collective-permute-start(bf16[1,32,320]{2,1,0:T(8,128)(2,1)} %get-tuple-element.160), channel_id=1, source_target_pairs={{1,0},{3,2},{5,4},{7,6},{9,8},{11,10},{13,12},{15,14},{17,16},{19,... | collective-permute-start | bytes 61448 | tf_op jit(solution)/shard_map/ppermute | solution.py:21
  363.9 22.7 %collective-permute-start.23 = (bf16[4,32,320]{2,1,0:T(8,128)(2,1)}, bf16[4,32,320]{2,1,0:T(8,128)(2,1)}, u32[]{:S(2)}, u32[]{:S(2)}) collective-permute-start(bf16[4,32,320]{2,1,0:T(8,128)(2,1)} %add_convert_fusion), channel_id=1, source_target_pairs={{2,0},{4,2},{6,4},{8,6},{10,8},{12,10},{14,12},{16,14},{18,16},{20... | collective-permute-start | bytes 245768 | tf_op jit(solution)/shard_map/ppermute | solution.py:39
  370.8 10.6 %collective-permute-start.24 = (bf16[4,32,320]{2,1,0:T(8,128)(2,1)S(1)}, bf16[4,32,320]{2,1,0:T(8,128)(2,1)S(1)}, u32[]{:S(2)}, u32[]{:S(2)}) collective-permute-start(bf16[4,32,320]{2,1,0:T(8,128)(2,1)S(1)} %get-tuple-element.225), channel_id=1, source_target_pairs={{0,16},{16,0},{2,18},{18,2},{4,20},{20,4},{6,22},{22,6},{8,24},{24... | collective-permute-start | bytes 245768 | tf_op jit(solution)/shard_map/ppermute | solution.py:33
  375.9 22.2 %copy-start.1 = (bf16[1,3,2,4,32,320]{5,4,3,2,1,0:T(8,128)(2,1)}, bf16[1,3,2,4,32,320]{5,4,3,2,1,0:T(8,128)(2,1)S(1)}, u32[]{:S(2)}) copy-start(bf16[1,3,2,4,32,320]{5,4,3,2,1,0:T(8,128)(2,1)S(1)} %fusion.55) | copy-start | bytes 1474564
  375.9 14.7 %collective-permute-start.15 = (bf16[4,32,320]{2,1,0:T(8,128)(2,1)S(1)}, bf16[4,32,320]{2,1,0:T(8,128)(2,1)S(1)}, u32[]{:S(2)}, u32[]{:S(2)}) collective-permute-start(bf16[4,32,320]{2,1,0:T(8,128)(2,1)S(1)} %get-tuple-element.226), channel_id=1, source_target_pairs={{0,2},{2,4},{4,6},{6,8},{8,10},{10,12},{12,14},{14,16},{16,18},{18... | collective-permute-start | bytes 245768 | tf_op jit(solution)/shard_map/ppermute | solution.py:39
  381.4 4.6 %collective-permute-start.25 = (bf16[4,32,320]{2,1,0:T(8,128)(2,1)S(1)}, bf16[4,32,320]{2,1,0:T(8,128)(2,1)S(1)}, u32[]{:S(2)}, u32[]{:S(2)}) collective-permute-start(bf16[4,32,320]{2,1,0:T(8,128)(2,1)S(1)} %collective-permute-done.24), channel_id=1, source_target_pairs={{0,8},{8,0},{2,10},{10,2},{4,12},{12,4},{6,14},{14,6},{16,24},{24,... | collective-permute-start | bytes 245768 | tf_op jit(solution)/shard_map/ppermute | solution.py:33
  386.1 4.6 %collective-permute-start.26 = (bf16[4,32,320]{2,1,0:T(8,128)(2,1)S(1)}, bf16[4,32,320]{2,1,0:T(8,128)(2,1)S(1)}, u32[]{:S(2)}, u32[]{:S(2)}) collective-permute-start(bf16[4,32,320]{2,1,0:T(8,128)(2,1)S(1)} %collective-permute-done.25), channel_id=1, source_target_pairs={{0,4},{4,0},{2,6},{6,2},{8,12},{12,8},{10,14},{14,10},{16,20},{20,... | collective-permute-start | bytes 245768 | tf_op jit(solution)/shard_map/ppermute | solution.py:33
  390.7 1.3 collective-permute-start.27
  (24 other events, 120.3 us)
Sparse Core Ops, SparseCore 0:
  10.2 62.1 all-gather.2
  308.8 61.4 reduce-scatter.1
where the time goes:
time: 409 us; the launch traced here: 405 us
  local copies, waits for them, and re-layouts  124 us (30%)
  starting transfers between devices  86.4 us (21%)
  other arithmetic  60.5 us (15%)
  waiting for transfers between devices  41.7 us (10%)
  between operations  32.6 us (8%)
  matrix products  30 us (7%)
  blocking collectives  29.2 us (7%)
    ppermute x12, starting transfers between devices, extended(): before = lax.ppermute(last, axis, up)  51.9 us
    all_gather x1, waiting for transfers between devices, per_device(): kernels = lax.all_gather(weights[0], 'row', axis=3, tiled=True)  25.4 us
    psum x4, blocking collectives, forward_norm(): lax.psum((jnp.sum(values, axis=(0, 2)), jnp.sum(values * values, axis=(0,...  23.6 us
    dot_general x8, matrix products, convolve_padded(): jnp.dot(patches(padded, row_tally, col_count), kernel.reshape(-1, kernel....  23.3 us
    concatenate x12, local copies, waits for them, and re-layouts, patches(): return jnp.concatenate(pieces, axis=2).reshape(row_tally * col_count, -1)  22.6 us
    dot_general x4, local copies, waits for them, and re-layouts, convolve_padded(): jnp.dot(patches(padded, row_tally, col_count), kernel.reshape(-1, kernel....  16.5 us
    ppermute x12, starting transfers between devices, extended(): after = lax.ppermute(initial, axis, down)  15.8 us
    ppermute x8, waiting for transfers between devices, partner_2(): return lax.ppermute(block, axis, route)  14.2 us
  transfers between devices with their start and end apart: 38, of which 8 were waited for; matrix products, arithmetic and copies ran while one was open for 37% of the time, Pallas kernels for 0%

commit v1 on v0

v1 whole, which is shorter than its diff:
```python
import functools

import jax
import jax.numpy as jnp
from jax import lax
from jax.experimental import pallas as pl
from jax.experimental.pallas import tpu as pltpu
from jax.sharding import PartitionSpec as P

GROUPS = 32
TICKS = 2
FOLD = 4
EPSILON = 1e-05
BF, F32 = jnp.bfloat16, jnp.float32
VMEM_LIMIT = 24 * 2**20


class Sizes:
    def __init__(self, queue, sections, rows):
        self.sections, self.parts = sections, rows
        self.cols = queue.shape[2]
        self.channels = queue.shape[3]
        self.local = queue.shape[1] * queue.shape[2]
        self.cells = self.local * rows
        self.share = self.channels // rows
        self.group = self.channels // GROUPS
        self.count = self.cells * self.group


def where_am_i():
    return lax.axis_index("section"), lax.axis_index("row")


def share_of(z, value, part):
    value = value.astype(F32)
    out = value[:, : z.share]
    for j in range(1, z.parts):
        out = jnp.where(part == j, value[:, j * z.share : (j + 1) * z.share], out)
    return out


def all_shares(z, own, others, row):
    out = []
    for j in range(z.parts):
        value = own
        for d in range(1, z.parts):
            value = jnp.where(lax.rem(row + z.parts - d, z.parts) == j, others[d - 1], value)
        out.append(value)
    return out


def side_by_side(values):
    return jnp.concatenate([value.astype(F32) for value in values], axis=1)


def fold(z, ref, value):
    rows = value.shape[0] // FOLD
    ref[...] = side_by_side([value[j * rows : (j + 1) * rows] for j in range(FOLD)]).astype(BF)


def unfold(z, ref):
    value = ref[...].astype(F32)
    return jnp.concatenate([value[:, j * z.share : (j + 1) * z.share] for j in range(FOLD)], axis=0)


def source(z, row, d):
    return lax.rem(row + z.parts - d, z.parts)


def target(z, row, d):
    return lax.rem(row + d, z.parts)


def part_rows(z, part):
    return pl.ds(pl.multiple_of(part * z.local, z.local), z.local)


def assemble(z, ref, pieces, row, start, width):
    for d, piece in enumerate(pieces):
        value = piece[...].astype(F32)[:, start : start + width]
        ref[part_rows(z, source(z, row, d)), :] = value.astype(BF)


def group_sums(z, first, second):
    width = first.shape[1]
    line = lax.broadcasted_iota(jnp.int32, (8, width), 0)
    both = jnp.where(line == 0, first, jnp.where(line == 1, second, 0.0))
    across = lax.broadcasted_iota(jnp.int32, (width, width), 1).astype(F32)
    down = lax.broadcasted_iota(jnp.int32, (width, width), 0).astype(F32)
    same = jnp.floor((across + 0.5) * (1.0 / z.group)) == jnp.floor((down + 0.5) * (1.0 / z.group))
    sums = jnp.dot(
        both, same.astype(F32), precision=lax.Precision.HIGHEST, preferred_element_type=F32
    )
    return sums[0:1], sums[1:2]


def normalize(z, x):
    total, square = group_sums(
        z, jnp.sum(x, axis=0, keepdims=True), jnp.sum(x * x, axis=0, keepdims=True)
    )
    center = total / z.count
    factor = lax.rsqrt(square / z.count - center * center + EPSILON)
    return (x - center) * factor, factor


def sigmoid(y):
    return 1.0 / (1.0 + jnp.exp(-y))


def norm_back(z, y, factor, logistic, upstream):
    e = upstream * logistic * (1.0 + y * (1.0 - logistic))
    first, second = group_sums(
        z, jnp.sum(e, axis=0, keepdims=True), jnp.sum(e * y, axis=0, keepdims=True)
    )
    return factor * (e - first / z.count - y * (second / z.count))


def spread(z, x, line_ref, pad_ref):
    cells, cols = z.cells, z.cols
    width = x.shape[1]
    line_ref[8 : 8 + cells, :] = x
    column = lax.rem(lax.broadcasted_iota(jnp.int32, (cells, 1), 0), cols)
    edge = jnp.zeros((cols, width), BF)
    for b in range(3):
        pad_ref[b, :cols, :] = edge
        pad_ref[b, cols + cells :, :] = edge
    pad_ref[1, cols : cols + cells, :] = x.astype(BF)
    left = jnp.where(column > 0, line_ref[7 : 7 + cells, :], 0.0)
    pad_ref[0, cols : cols + cells, :] = left.astype(BF)
    right = jnp.where(column < cols - 1, line_ref[9 : 9 + cells, :], 0.0)
    pad_ref[2, cols : cols + cells, :] = right.astype(BF)


def convolve(z, pad_ref, kernel_ref):
    total = None
    for a in range(3):
        for b in range(3):
            term = jnp.dot(
                pad_ref[b, a * z.cols : a * z.cols + z.cells, :],
                kernel_ref[3 * a + b],
                preferred_element_type=F32,
            )
            total = term if total is None else total + term
    return total


def convolve_back(z, pad_ref, kernel_ref):
    total = None
    for a in range(3):
        for b in range(3):
            term = lax.dot_general(
                pad_ref[b, a * z.cols : a * z.cols + z.cells, :],
                kernel_ref[3 * (2 - a) + 2 - b],
                (((1,), (1,)), ((), ())),
                preferred_element_type=F32,
            )
            total = term if total is None else total + term
    return total


def pad_shapes(z, width):
    return [
        pltpu.VMEM((z.cells + 16, width), F32),
        pltpu.VMEM((3, z.cells + 2 * z.cols, width), BF),
    ]


def call(body, name, scalars, arrays, outs, scratch=(), flops=0):
    moved = sum(x.size * x.dtype.itemsize for x in arrays)
    return pl.pallas_call(
        body,
        name=name,
        out_shape=[jax.ShapeDtypeStruct(shape, dtype) for shape, dtype in outs],
        in_specs=[pl.BlockSpec(memory_space=pltpu.SMEM)] * len(scalars)
        + [pl.BlockSpec(memory_space=pltpu.VMEM)] * len(arrays),
        out_specs=[pl.BlockSpec(memory_space=pltpu.VMEM)] * len(outs),
        scratch_shapes=list(scratch),
        compiler_params=pltpu.CompilerParams(vmem_limit_bytes=VMEM_LIMIT),
        cost_estimate=pl.CostEstimate(flops=flops, bytes_accessed=moved, transcendentals=0),
    )(*scalars, *arrays)


def pack_first(z, fs, bs, fwd, bwd, mir, stash, *outs):
    s, row = where_am_i()
    f, b = fs[0, s], bs[0, s]
    h, i = fwd[f], stash[2 * b + 1]
    g = bwd[b].astype(F32) + jnp.where(s < z.sections // 2, mir[b].astype(F32), 0.0)
    for d, out in enumerate(outs):
        part = target(z, row, d)
        out[...] = side_by_side([share_of(z, h, part), share_of(z, i, part), g]).astype(BF)


def pack_second(z, fs, bs, fwd, bwd, mir, stash, *outs):
    s, row = where_am_i()
    encoder = s < z.sections // 2
    f0, f1, b0, b1 = fs[0, s], fs[1, s], bs[0, s], bs[1, s]
    w = z.share
    halves = (stash[2 * b0], fwd[f1], stash[2 * b1], stash[2 * b1 + 1])
    skip_back, skip_now, skip_before = mir[b1].astype(F32), mir[f1], mir[f0]
    for d, out in enumerate(outs):
        part = target(z, row, d)
        values = [share_of(z, value, part) for value in halves] + [bwd[b1]]
        values.append(jnp.where(encoder, skip_back[:, :w], share_of(z, skip_now, part)))
        values.append(jnp.where(encoder, skip_back[:, w : 2 * w], share_of(z, skip_before, part)))
        if z.parts > 2:
            values.append(skip_back[:, 2 * w :])
        out[...] = side_by_side(values).astype(BF)


def send_partials(z, row, total, own, sends):
    own[...] = share_of(z, total, row)
    for d, send in enumerate(sends, 1):
        fold(z, send, share_of(z, total, target(z, row, d)))


def first_forward(z, *refs):
    n = z.parts
    pieces, kernel, (own, h_out), sends = refs[:n], refs[n], refs[n + 1 : n + 3], refs[n + 3 : 2 * n + 2]
    line, pad = refs[2 * n + 2 :]
    _, row = where_am_i()
    assemble(z, h_out, pieces, row, 0, z.share)
    y, _ = normalize(z, h_out[...].astype(F32))
    spread(z, y * sigmoid(y), line, pad)
    send_partials(z, row, convolve(z, pad, kernel), own, sends)


def later_forward(z, fs, *refs):
    n = z.parts
    arrivals, pieces, kernel = refs[:n], refs[n : 2 * n], refs[2 * n]
    own, h_out, arrived = refs[2 * n + 1 : 2 * n + 4]
    sends = refs[2 * n + 4 : 3 * n + 3]
    line, pad = refs[3 * n + 3 :]
    s, row = where_am_i()
    total = unfold(z, arrivals[0])
    for other in arrivals[1:]:
        total = total + unfold(z, other)
    total = total.astype(BF).astype(F32)
    arrived[...] = total.astype(BF)
    assemble(z, h_out, pieces, row, z.share, z.share)
    prior = jnp.maximum(s - 1, 0)
    taken = jnp.logical_and(s > 0, fs[0, prior] == fs[1, s])
    h = jnp.where(taken, total, h_out[...].astype(F32))
    h_out[...] = h.astype(BF)
    y, _ = normalize(z, h)
    spread(z, y * sigmoid(y), line, pad)
    send_partials(z, row, convolve(z, pad, kernel), own, sends)


def back_through_second(z, i, g, kernel, q_out, q_send, act_out, line, pad):
    y, factor = normalize(z, i.astype(F32))
    logistic = sigmoid(y)
    act_out[...] = (y * logistic).astype(BF)
    spread(z, g, line, pad)
    q = norm_back(z, y, factor, logistic, convolve_back(z, pad, kernel)).astype(BF)
    q_out[...] = q
    fold(z, q_send, q.astype(F32))


def first_backward(z, *refs):
    n = z.parts
    pieces, kernel = refs[:n], refs[n]
    q_out, q_send, g_out, act_out, i_ref, line, pad = refs[n + 1 :]
    _, row = where_am_i()
    assemble(z, i_ref, pieces, row, z.share, z.share)
    assemble(z, g_out, pieces, row, 2 * z.share, z.channels)
    back_through_second(
        z, i_ref[...], g_out[...].astype(F32), kernel, q_out, q_send, act_out, line, pad
    )


def later_backward(z, fs, bs, *refs):
    n = z.parts
    arrivals, mirrors, pieces = refs[:n], refs[n : 2 * n], refs[2 * n : 3 * n]
    i_before, kernel = refs[3 * n : 3 * n + 2]
    q_out, q_send, g_out, act_out, grad_in, skip_in, i_ref, full, line, pad = refs[3 * n + 2 :]
    s, row = where_am_i()
    encoder = s < z.sections // 2
    w = z.share
    for out, parts in ((grad_in, arrivals), (skip_in, mirrors)):
        shares = [unfold(z, part) for part in parts]
        out[...] = side_by_side(all_shares(z, shares[0], shares[1:], row)).astype(BF)
    later = jnp.minimum(s + 1, z.sections - 1)
    partner = z.sections - 1 - s
    grad_taken = jnp.logical_and(s < z.sections - 1, bs[0, later] == bs[1, s])
    skip_taken = bs[0, partner] == bs[1, s]
    assemble(z, full, pieces, row, 4 * w, z.channels)
    g = jnp.where(grad_taken, grad_in[...].astype(F32), full[...].astype(F32))
    assemble(z, full, pieces, row, 4 * w + z.channels, z.channels)
    skip = jnp.where(skip_taken, skip_in[...].astype(F32), full[...].astype(F32))
    g_out[...] = (g + jnp.where(encoder, skip, 0.0)).astype(BF)
    assemble(z, i_ref, pieces, row, 3 * w, w)
    i = jnp.where(fs[0, s] == bs[1, s], i_before[...].astype(F32), i_ref[...].astype(F32))
    back_through_second(
        z, i, g_out[...].astype(F32), kernel, q_out, q_send, act_out, line, pad
    )


def second_convolution(z, encoder, row, own, received, skip, h, kernel, i_out, full, line, pad):
    c0 = own[...]
    for other in received:
        c0 = c0 + unfold(z, other)
    i = jnp.where(encoder, c0, skip.astype(F32)).astype(BF)
    i_out[...] = i
    y, _ = normalize(z, i.astype(F32))
    spread(z, y * sigmoid(y), line, pad)
    total = convolve(z, pad, kernel)
    base = h[...].astype(F32) + jnp.where(encoder, 0.0, c0)
    full[...] = total + side_by_side([jnp.where(row == j, base, 0.0) for j in range(z.parts)])


def second_forward(z, *refs):
    n = z.parts
    own, received, h = refs[0], refs[1:n], refs[n]
    pieces, q, kernel = refs[n + 1 : 2 * n + 1], refs[2 * n + 1], refs[2 * n + 2]
    i_out, full_out = refs[2 * n + 3 : 2 * n + 5]
    sends, mirrors = refs[2 * n + 5 : 3 * n + 5], refs[3 * n + 5 : 4 * n + 5]
    skip, full, line, pad = refs[4 * n + 5 :]
    s, row = where_am_i()
    encoder = s < z.sections // 2
    assemble(z, skip, pieces, row, 5 * z.share + z.channels, z.share)
    second_convolution(
        z, encoder, row, own, received, skip[...], h, kernel, i_out, full, line, pad
    )
    full_out[...] = full[...].astype(BF)
    q_now = q[...].astype(F32)
    for d in range(n):
        piece = share_of(z, full[...], target(z, row, d))
        fold(z, sends[d], piece)
        fold(z, mirrors[d], jnp.where(encoder, piece, q_now))


def last_forward(z, fs, *refs):
    n = z.parts
    own, received, h = refs[0], refs[1:n], refs[n]
    pieces, arrived, kernel = refs[n + 1 : 2 * n + 1], refs[2 * n + 1], refs[2 * n + 2]
    sends = refs[2 * n + 3 : 3 * n + 3]
    i_out, skip, full, line, pad = refs[3 * n + 3 :]
    s, row = where_am_i()
    encoder = s < z.sections // 2
    partner = z.sections - 1 - s
    assemble(z, skip, pieces, row, 4 * z.share + z.channels, z.share)
    now = jnp.where(
        fs[0, partner] == fs[1, s], arrived[...].astype(F32), skip[...].astype(F32)
    )
    second_convolution(z, encoder, row, own, received, now, h, kernel, i_out, full, line, pad)
    for d, send in enumerate(sends):
        at = part_rows(z, target(z, row, d))
        send[...] = side_by_side([full[at, :], i_out[at, :]]).astype(BF)


def back_through_first(z, encoder, row, q, received, g, h, kernel, grad_out, act_out, line, pad):
    shares = all_shares(z, q[...].astype(F32), [unfold(z, other) for other in received], row)
    whole = side_by_side(shares)
    now = jnp.where(encoder, whole, g[...].astype(F32))
    grad_out[...] = now.astype(BF)
    y, factor = normalize(z, h.astype(F32))
    logistic = sigmoid(y)
    act_out[...] = (y * logistic).astype(BF)
    spread(z, now, line, pad)
    back = norm_back(z, y, factor, logistic, convolve_back(z, pad, kernel))
    return share_of(z, g[...], row) + back, whole


def second_backward(z, *refs):
    n = z.parts
    q, received, g, pieces, kernel = refs[0], refs[1:n], refs[n], refs[n + 1 : 2 * n + 1], refs[2 * n + 1]
    send, grad_out, act_out, h, line, pad = refs[2 * n + 2 :]
    s, row = where_am_i()
    assemble(z, h, pieces, row, 0, z.share)
    value, _ = back_through_first(
        z, s < z.sections // 2, row, q, received, g, h[...], kernel, grad_out, act_out, line, pad
    )
    fold(z, send, value)


def last_backward(z, fs, bs, *refs):
    n = z.parts
    q, received, g, pieces = refs[0], refs[1:n], refs[n], refs[n + 1 : 2 * n + 1]
    h_before, kernel = refs[2 * n + 1 : 2 * n + 3]
    sends = refs[2 * n + 3 : 3 * n + 3]
    q_rows, grad_out, act_out, h, value, whole, line, pad = refs[3 * n + 3 :]
    s, row = where_am_i()
    assemble(z, h, pieces, row, 2 * z.share, z.share)
    now = jnp.where(fs[0, s] == bs[1, s], h_before[...], h[...])
    result, entered = back_through_first(
        z, s < z.sections // 2, row, q, received, g, now, kernel, grad_out, act_out, line, pad
    )
    value[...] = result.astype(BF)
    for d, send in enumerate(sends):
        fold(z, send, value[part_rows(z, target(z, row, d)), :])
    whole[...] = entered.astype(BF)
    q_rows[...] = whole[part_rows(z, row), :]


def pack_rows(z, *refs):
    n = z.parts
    full, i, arrived, mirrors = refs[0], refs[1], refs[2], refs[3 : n + 3]
    sends, skip = refs[n + 3 : 2 * n + 3], refs[2 * n + 3]
    _, row = where_am_i()
    total = unfold(z, mirrors[0])
    for other in mirrors[1:]:
        total = total + unfold(z, other)
    skip[...] = total.astype(BF)
    for d, send in enumerate(sends):
        at = part_rows(z, target(z, row, d))
        send[...] = side_by_side([ref[at, :] for ref in (full, i, arrived, skip)]).astype(BF)


def add_rows(z, *refs):
    n = z.parts
    pieces, q_rows = refs[:n], refs[n]
    out, mirror, i_rows = refs[n + 1 :]
    s, row = where_am_i()
    c = z.channels
    values = [piece[...].astype(F32) for piece in pieces]
    total = sum(value[:, :c] for value in values)
    out[...] = total.astype(BF)
    mirror[...] = jnp.where(s < z.sections // 2, total, q_rows[...].astype(F32)).astype(BF)
    shares = all_shares(z, values[0][:, c:], [value[:, c:] for value in values[1:]], row)
    i_rows[...] = side_by_side(shares).astype(BF)


def finish(z, fs, bs, *refs):
    n = z.parts
    fwd, bwd, mir, stash = refs[:4]
    rows0 = refs[4 : n + 4]
    grad_in, skip_in, out1, i1, fwd1, mir1 = refs[n + 4 : n + 10]
    grads1 = refs[n + 10 : 2 * n + 10]
    fwd_out, bwd_out, mir_out, stash_out, emitted = refs[2 * n + 10 :]
    s, row = where_am_i()
    encoder = s < z.sections // 2
    c, w = z.channels, z.share
    prior, later = jnp.maximum(s - 1, 0), jnp.minimum(s + 1, z.sections - 1)
    partner = z.sections - 1 - s
    has_prior, has_later = s > 0, s < z.sections - 1
    mine = part_rows(z, row)

    pieces = [piece[...].astype(F32) for piece in rows0]

    def joined(at):
        shares = [piece[:, at : at + w] for piece in pieces]
        return side_by_side(all_shares(z, shares[0], shares[1:], row))

    total = sum(piece[:, :c] for piece in pieces)
    emitted[0] = total.astype(BF)
    emitted[1] = out1[...]

    i0 = joined(c)
    stash_out[...] = stash[...]
    f0, f1 = fs[0, s], fs[1, s]
    stash_out[2 * f0] = fwd[f0]
    stash_out[2 * f0 + 1] = i0.astype(BF)
    fwd_in = joined(c + w)
    taken = jnp.logical_and(has_prior, fs[0, prior] == f1)
    stash_out[2 * f1] = jnp.where(taken, fwd_in, fwd[f1].astype(F32)).astype(BF)
    stash_out[2 * f1 + 1] = i1[...]

    fwd_out[...] = fwd[...]

    @pl.when(has_prior)
    def _():
        fwd_out[fs[0, prior]] = fwd_in.astype(BF)
        fwd_out[fs[1, prior]] = fwd1[...]

    mir_out[...] = mir[...]
    skip = jnp.where(encoder, skip_in[mine, :].astype(F32), joined(c + 2 * w))
    mir_out[jnp.where(encoder, bs[0, partner], fs[0, partner])] = skip.astype(BF)
    mir_out[jnp.where(encoder, bs[1, partner], fs[1, partner])] = mir1[...]

    bwd_out[...] = bwd[...]
    shares = [unfold(z, piece) for piece in grads1]
    grads = side_by_side(all_shares(z, shares[0], shares[1:], row)).astype(BF)

    @pl.when(has_later)
    def _():
        bwd_out[bs[0, later]] = grad_in[mine, :]
        bwd_out[bs[1, later]] = grads


def kernel_grads(z, acts0, acts1, grads0, grads1, acts2, acts3, grads2, grads3, acc, out, turned, line, pad):
    step = pl.program_id(0)

    def prepare(acts, grads):
        for t in range(TICKS):
            turned[t] = jnp.transpose(acts[t][...].astype(F32)).astype(BF)
            spread(z, grads[t][...].astype(F32), line, pad.at[t])

    @pl.when(step == 0)
    def _():
        prepare((acts0, acts1), (grads0, grads1))

    @pl.when(step == 9)
    def _():
        prepare((acts2, acts3), (grads2, grads3))

    tap = lax.rem(step, 9)
    a, b = lax.div(tap, 3), lax.rem(tap, 3)
    at = pl.ds(pl.multiple_of((2 - a) * z.cols, z.cols), z.cells)
    total = acc[0]
    for t in range(TICKS):
        total = total + jnp.dot(turned[t], pad[t, 2 - b, at, :], preferred_element_type=F32)
    out[0] = total


def per_device(fwd_queue, bwd_queue, mirror_queue, stash, weights, grad_acc, fwd_slot, bwd_slot):
    sections, n = lax.axis_size("section"), lax.axis_size("row")
    z = Sizes(fwd_queue[0], sections, n)
    slots = fwd_queue.shape[1]
    c, w, local, cells = z.channels, z.share, z.local, z.cells
    fwd, bwd, mir = (x.reshape(slots, local, c) for x in (fwd_queue, bwd_queue, mirror_queue))
    kept = stash.reshape(2 * slots, local, c)
    kernels = weights.reshape(2, 9, w, c)
    first_kernel, second_kernel = kernels[0], kernels[1]
    fs, bs = fwd_slot.T, bwd_slot.T
    folded, wide = (cells // FOLD, FOLD * w), (cells, c)
    half = (cells, w)
    flops = 2 * cells * 9 * w * c

    def move(x, d, step):
        route = [
            (s * n + r, step(s) * n + (r + d) % n) for s in range(sections) for r in range(n)
        ]
        return lax.ppermute(x, ("section", "row"), route)

    across = functools.partial(move, step=lambda s: s)
    onward = functools.partial(move, step=lambda s: (s + 1) % sections)
    backward = functools.partial(move, step=lambda s: (s - 1) % sections)
    mirrored = functools.partial(move, step=lambda s: sections - 1 - s)

    def run(body, scalars, arrays, outs, scratch=(), flops=0):
        return call(functools.partial(body, z), body.__name__, scalars, arrays, outs, scratch, flops)

    def exchange(pieces):
        return [pieces[0]] + [across(piece, d) for d, piece in enumerate(pieces[1:], 1)]

    narrow_pad, wide_pad = pad_shapes(z, w), pad_shapes(z, c)
    queues = (fwd, bwd, mir, kept)
    first = exchange(run(pack_first, (fs, bs), queues, [((local, 2 * w + c), BF)] * n))
    second = exchange(run(pack_second, (fs, bs), queues, [((local, 4 * w + 2 * c), BF)] * n))

    own, h0, *sends = run(
        first_forward,
        (),
        (*first, first_kernel),
        [(half, F32), (half, BF)] + [(folded, BF)] * (n - 1),
        narrow_pad,
        flops,
    )
    received = [across(x, d) for d, x in enumerate(sends, 1)]
    q0, q_send, g0, act_i0 = run(
        first_backward,
        (),
        (*first, second_kernel),
        [(half, BF), (folded, BF), (wide, BF), (half, BF)],
        [pltpu.VMEM(half, BF)] + wide_pad,
        flops,
    )
    q_received = [across(q_send, d) for d in range(1, n)]
    i0, full0, *sends = run(
        second_forward,
        (),
        (own, *received, h0, *second, q0, second_kernel),
        [(half, BF), (wide, BF)] + [(folded, BF)] * (2 * n),
        [pltpu.VMEM(half, BF), pltpu.VMEM(wide, F32)] + narrow_pad,
        flops,
    )
    fwd_in = [onward(x, d) for d, x in enumerate(sends[:n])]
    mir_in = [mirrored(x, d) for d, x in enumerate(sends[n:])]
    dh_send, grad0, act_h0 = run(
        second_backward,
        (),
        (q0, *q_received, g0, *second, first_kernel),
        [(folded, BF), (wide, BF), (half, BF)],
        [pltpu.VMEM(half, BF)] + wide_pad,
        flops,
    )
    dh_in = [backward(dh_send, d) for d in range(n)]

    own, h1, arrived, *sends = run(
        later_forward,
        (fs,),
        (*fwd_in, *second, first_kernel),
        [(half, F32), (half, BF), (half, BF)] + [(folded, BF)] * (n - 1),
        narrow_pad,
        flops,
    )
    received = [across(x, d) for d, x in enumerate(sends, 1)]
    q1, q_send, g1, act_i1, grad_in, skip_in = run(
        later_backward,
        (fs, bs),
        (*dh_in, *mir_in, *second, i0, second_kernel),
        [(half, BF), (folded, BF), (wide, BF), (half, BF), (wide, BF), (wide, BF)],
        [pltpu.VMEM(half, BF), pltpu.VMEM(wide, BF)] + wide_pad,
        flops,
    )
    q_received = [across(q_send, d) for d in range(1, n)]
    *sends, skip_arrived = run(
        pack_rows,
        (),
        (full0, i0, arrived, *mir_in),
        [((local, c + 3 * w), BF)] * n + [(half, BF)],
    )
    rows0 = exchange(sends)
    sends = run(
        last_forward,
        (fs,),
        (own, *received, h1, *second, skip_arrived, second_kernel),
        [((local, c + w), BF)] * n,
        [pltpu.VMEM(half, BF), pltpu.VMEM(half, BF), pltpu.VMEM(wide, F32)] + narrow_pad,
        flops,
    )
    rows1 = exchange(sends)
    *dh_sends, q_rows, grad1, act_h1 = run(
        last_backward,
        (fs, bs),
        (q1, *q_received, g1, *second, h0, first_kernel),
        [((local // FOLD, FOLD * w), BF)] * n + [((local, c), BF), (wide, BF), (half, BF)],
        [pltpu.VMEM(half, BF), pltpu.VMEM(half, BF), pltpu.VMEM(wide, BF)] + wide_pad,
        flops,
    )
    dh1_in = [backward(x, d) for d, x in enumerate(dh_sends)]
    out1, mirror1, i1 = run(add_rows, (), (*rows1, q_rows), [((local, c), BF)] * 3)
    fwd1, mir1 = onward(out1, 0), mirrored(mirror1, 0)

    whole = pl.BlockSpec(memory_space=pltpu.VMEM)
    tap = pl.BlockSpec((1, w, c), lambda i: (i, 0, 0))
    grad_total = pl.pallas_call(
        functools.partial(kernel_grads, z),
        name="kernel_grads",
        grid=(18,),
        out_shape=jax.ShapeDtypeStruct((18, w, c), F32),
        in_specs=[whole] * 8 + [tap],
        out_specs=tap,
        scratch_shapes=[
            pltpu.VMEM((TICKS, w, cells), BF),
            pltpu.VMEM((cells + 16, c), F32),
            pltpu.VMEM((TICKS, 3, cells + 2 * z.cols, c), BF),
        ],
        compiler_params=pltpu.CompilerParams(vmem_limit_bytes=VMEM_LIMIT),
        cost_estimate=pl.CostEstimate(
            flops=4 * flops, bytes_accessed=2 * grad_acc.size * 4, transcendentals=0
        ),
    )(act_h0, act_h1, grad0, grad1, act_i0, act_i1, g0, g1, grad_acc.reshape(18, w, c))

    fwd_out, bwd_out, mir_out, stash_out, emitted = run(
        finish,
        (fs, bs),
        (*queues, *rows0, grad_in, skip_in, out1, i1, fwd1, mir1, *dh1_in),
        [((slots, local, c), BF)] * 3 + [((2 * slots, local, c), BF), ((TICKS, local, c), BF)],
    )
    return (
        fwd_out.reshape(fwd_queue.shape),
        bwd_out.reshape(bwd_queue.shape),
        mir_out.reshape(mirror_queue.shape),
        stash_out.reshape(stash.shape),
        grad_total.reshape(grad_acc.shape),
        emitted.reshape((1, TICKS) + fwd_queue.shape[2:]),
    )


def solution(mesh):
    return jax.shard_map(
        per_device,
        mesh=mesh,
        in_specs=(
            P("section", None, "row", None, None),
            P("section", None, "row", None, None),
            P("section", None, "row", None, None),
            P("section", None, None, "row", None, None),
            P("section", None, None, None, "row", None),
            P("section", None, None, None, "row", None),
            P(),
            P(),
        ),
        out_specs=(
            P("section", None, "row", None, None),
            P("section", None, "row", None, None),
            P("section", None, "row", None, None),
            P("section", None, None, "row", None, None),
            P("section", None, None, None, "row", None),
            P("section", None, "row", None, None),
        ),
        check_vma=False,
    )
```

time: 409 us -> 72.8 us (0.18)
  local copies, waits for them, and re-layouts: 124 us -> 5.56 us
  other arithmetic: 60.5 us -> 0.01 us
  starting transfers between devices: 86.4 us -> 26 us
  between operations: 32.6 us -> 0.86 us
  waiting for transfers between devices: 41.7 us -> 10.9 us
  matrix products: 30 us -> 0 us
  blocking collectives: 29.2 us -> 0 us
  Pallas kernels: 0 us -> 28.8 us
    ppermute x36 -> x18, starting transfers between devices: 86.4 us -> 26 us  [move(): return lax.ppermute(x, ('section', 'row'), route)]
    dot_general x10 -> x0, matrix products: 30 us -> none  [the longest x8 23.3 us: convolve_padded(): jnp.dot(patches(padded, row_tally, col_count), kernel.reshape(-1, kernel....]
    psum x5 -> x0, blocking collectives: 29.2 us -> none  [the longest x4 23.6 us: forward_norm(): lax.psum((jnp.sum(values, axis=(0, 2)), jnp.sum(values * values, axis=(0,...]
    pallas_call x0 -> x14, Pallas kernels: none -> 28.8 us  [the longest x13 19.3 us: call(): pl.pallas_call(body, name=name, out_shape=[jax.ShapeDtypeStruct(shape, dt...]
    all_gather x1 -> x0, waiting for transfers between devices: 25.4 us -> none  [per_device(): kernels = lax.all_gather(weights[0], 'row', axis=3, tiled=True)]
    concatenate x12 -> x0, local copies, waits for them, and re-layouts: 22.6 us -> none  [patches(): return jnp.concatenate(pieces, axis=2).reshape(row_tally * col_count, -1)]
    convert_element_type x18 -> x0, local copies, waits for them, and re-layouts: 17.9 us -> none  [the longest x8 10.2 us: grouped(): tensor.astype(jnp.float32).reshape(-1, GROUPS, tensor.shape[-1] // GROUPS)]
    dot_general x4 -> x0, local copies, waits for them, and re-layouts: 16.5 us -> none  [convolve_padded(): jnp.dot(patches(padded, row_tally, col_count), kernel.reshape(-1, kernel....]
  transfers between devices with their start and end apart: 38 -> 18, of which waited for: 8 -> 3; matrix products, arithmetic and copies ran while one was open for 37% -> 0% of each run, Pallas kernels for 0% -> 34%
where the time goes in v1:
time: 72.8 us; the launch traced here: 72.2 us
  Pallas kernels  28.8 us (40%)
  starting transfers between devices  26 us (36%)
  waiting for transfers between devices  10.9 us (15%)
  local copies, waits for them, and re-layouts  5.56 us (8%)
  between operations  0.86 us (1%)
    ppermute x18, starting transfers between devices, move(): return lax.ppermute(x, ('section', 'row'), route)  26 us
    pallas_call x13, Pallas kernels, call(): pl.pallas_call(body, name=name, out_shape=[jax.ShapeDtypeStruct(shape, dt...  19.3 us
    ppermute x18, waiting for transfers between devices, move(): return lax.ppermute(x, ('section', 'row'), route)  10.9 us
    pallas_call x1, Pallas kernels, per_device(): pl.pallas_call(functools.partial(kernel_grads, z), name='kernel_grads', g...  9.54 us
    unnamed x26, local copies, waits for them, and re-layouts  5.34 us
  transfers between devices with their start and end apart: 18, of which 3 were waited for; matrix products, arithmetic and copies ran while one was open for 0% of the time, Pallas kernels for 34%

profile of v1, /device:TPU:0, one launch (start us, length us, event | category | flops | bytes accessed | tf_op | source)
XLA Modules:
  0.0 72.2 jit_solution(4332870118066232545)
XLA Ops:
  0.6 0.0 copy-start
  0.6 1.1 %copy-done = bf16[1,3,2,4,32,320]{5,4,3,2,1,0:T(8,128)(2,1)S(1)} copy-done((bf16[1,3,2,4,32,320]{5,4,3,2,1,0:T(8,128)(2,1)S(1)}, bf16[1,3,2,4,32,320]{5,4,3,2,1,0:T(8,128)(2,1)}, u32[]{:S(2)}) %copy-start) | copy-done | bytes 491544
  1.7 1.0 %copy-done.2 = bf16[1,3,4,32,320]{4,3,2,1,0:T(8,128)(2,1)S(1)} copy-done((bf16[1,3,4,32,320]{4,3,2,1,0:T(8,128)(2,1)S(1)}, bf16[1,3,4,32,320]{4,3,2,1,0:T(8,128)(2,1)}, u32[]{:S(2)}) %copy-start.2) | copy-done | bytes 245784
  2.7 1.0 %copy-done.4 = bf16[1,3,4,32,320]{4,3,2,1,0:T(8,128)(2,1)S(1)} copy-done((bf16[1,3,4,32,320]{4,3,2,1,0:T(8,128)(2,1)S(1)}, bf16[1,3,4,32,320]{4,3,2,1,0:T(8,128)(2,1)}, u32[]{:S(2)}) %copy-start.4) | copy-done | bytes 245784
  3.6 1.0 %copy-done.6 = bf16[1,3,4,32,320]{4,3,2,1,0:T(8,128)(2,1)S(1)} copy-done((bf16[1,3,4,32,320]{4,3,2,1,0:T(8,128)(2,1)S(1)}, bf16[1,3,4,32,320]{4,3,2,1,0:T(8,128)(2,1)}, u32[]{:S(2)}) %copy-start.6) | copy-done | bytes 245784
  4.6 0.7 copy-done.8
  5.3 0.7 copy-done.9
  5.9 0.7 %pack_first.1 = (bf16[128,640]{1,0:T(8,128)(2,1)S(1)}, bf16[128,640]{1,0:T(8,128)(2,1)S(1)}) custom-call(s32[2,16]{1,0:T(2,128)S(1)} %bitcast.38, s32[2,16]{1,0:T(2,128)S(1)} %bitcast.45, bf16[3,128,320]{2,1,0:T(8,128)(2,1)S(1)} %bitcast.29, bf16[3,128,320]{2,1,0:T(8,128)(2,1)S(1)} %bitcast.32, bf16[3,128,320]{2,1,0:T(8,128)(2,1)S(1)} %bitcast.35, ...), custom_call_target="tpu_custom_call" | custom-call | bytes 1228800 | tf_op jit(solution)/shard_map/pack_first/pallas_call | solution.py:170
  6.7 3.0 %collective-permute-start = (bf16[128,640]{1,0:T(8,128)(2,1)S(1)}, bf16[128,640]{1,0:T(8,128)(2,1)S(1)}, u32[]{:S(2)}, u32[]{:S(2)}) collective-permute-start(bf16[128,640]{1,0:T(8,128)(2,1)S(1)} %get-tuple-element.55), channel_id=1, source_target_pairs={{0,1},{1,0},{2,3},{3,2},{4,5},{5,4},{6,7},{7,6},{8,9},{9,8},{10,11... | collective-permute-start | bytes 491528 | tf_op jit(solution)/shard_map/ppermute | solution.py:523
  9.7 1.1 %pack_second.1 = (bf16[128,1280]{1,0:T(8,128)(2,1)S(1)}, bf16[128,1280]{1,0:T(8,128)(2,1)S(1)}) custom-call(s32[2,16]{1,0:T(2,128)S(1)} %bitcast.39, s32[2,16]{1,0:T(2,128)S(1)} %bitcast.46, bf16[3,128,320]{2,1,0:T(8,128)(2,1)S(1)} %bitcast.30, bf16[3,128,320]{2,1,0:T(8,128)(2,1)S(1)} %bitcast.33, bf16[3,128,320]{2,1,0:T(8,128)(2,1)S(1)} %bitcast.36, ...), custom_call_target="tpu_custom_call" | custom-call | bytes 1228800 | tf_op jit(solution)/shard_map/pack_second/pallas_call | solution.py:170
  10.8 0.1 collective-permute-start.2
  10.9 0.2 fusion
  11.1 3.6 %collective-permute-done.refs_1_ = bf16[128,640]{1,0:T(8,128)(2,1)S(1)} collective-permute-done((bf16[128,640]{1,0:T(8,128)(2,1)S(1)}, bf16[128,640]{1,0:T(8,128)(2,1)S(1)}, u32[]{:S(2)}, u32[]{:S(2)}) %collective-permute-start) | collective-permute-done | bytes 163872 | tf_op jit(solution)/shard_map/ppermute | solution.py:523
  14.8 1.4 %first_forward.1 = (f32[256,160]{1,0:T(8,128)S(1)}, bf16[256,160]{1,0:T(8,128)(2,1)S(1)}, bf16[64,640]{1,0:T(8,128)(2,1)S(1)}) custom-call(bf16[128,640]{1,0:T(8,128)(2,1)S(1)} %get-tuple-element.54.refs_0_, bf16[128,640]{1,0:T(8,128)(2,1)S(1)} %collective-permute-done.refs_1_, bf16[9,160,320]{2,1,0:T(8,128)(2,1)S(1)} %bitcast.15), custom_call_target="tpu_custom_call" | custom-call | flops 235929600 | bytes 1249280 | tf_op jit(solution)/shard_map/first_forward/pallas_call | solution.py:170
  16.2 2.1 %collective-permute-start.1 = (bf16[64,640]{1,0:T(8,128)(2,1)S(1)}, bf16[64,640]{1,0:T(8,128)(2,1)S(1)}, u32[]{:S(2)}, u32[]{:S(2)}) collective-permute-start(bf16[64,640]{1,0:T(8,128)(2,1)S(1)} %get-tuple-element.57), channel_id=1, source_target_pairs={{0,1},{1,0},{2,3},{3,2},{4,5},{5,4},{6,7},{7,6},{8,9},{9,8},{10,11... | collective-permute-start | bytes 245768 | tf_op jit(solution)/shard_map/ppermute | solution.py:523
  18.3 1.5 %first_backward.1 = (bf16[256,160]{1,0:T(8,128)(2,1)S(1)}, bf16[64,640]{1,0:T(8,128)(2,1)S(1)}, bf16[256,320]{1,0:T(8,128)(2,1)S(1)}, bf16[256,160]{1,0:T(8,128)(2,1)S(1)}) custom-call(bf16[128,640]{1,0:T(8,128)(2,1)S(1)} %get-tuple-element.54.refs_0_, bf16[128,640]{1,0:T(8,128)(2,1)S(1)} %collective-permute-done.refs_1_, bf16[9,160,320]{2,1,0:T(8,128)(2,1)S(1)} %bitcast.19), custom_call_target="tpu_custom_call" | custom-call | flops 235929600 | bytes 1249280 | tf_op jit(solution)/shard_map/first_backward/pallas_call | solution.py:170
  19.8 2.9 %collective-permute-done.1.refs_1_ = bf16[64,640]{1,0:T(8,128)(2,1)S(1)} collective-permute-done((bf16[64,640]{1,0:T(8,128)(2,1)S(1)}, bf16[64,640]{1,0:T(8,128)(2,1)S(1)}, u32[]{:S(2)}, u32[]{:S(2)}) %collective-permute-start.1) | collective-permute-done | bytes 81952 | tf_op jit(solution)/shard_map/ppermute | solution.py:523
  22.7 1.6 %second_forward.1 = (bf16[256,160]{1,0:T(8,128)(2,1)S(1)}, bf16[256,320]{1,0:T(8,128)(2,1)S(1)}, bf16[64,640]{1,0:T(8,128)(2,1)S(1)}, bf16[64,640]{1,0:T(8,128)(...) custom-call(f32[256,160]{1,0:T(8,128)S(1)} %get-tuple-element.56.refs_0_, ...), custom_call_target="tpu_custom_call" | custom-call | flops 235929600 | bytes 1986560 | tf_op jit(solution)/shard_map/second_forward/pallas_call | solution.py:170
  24.4 0.1 collective-permute-start.3
  24.4 2.9 %collective-permute-start.4 = (bf16[64,640]{1,0:T(8,128)(2,1)S(1)}, bf16[64,640]{1,0:T(8,128)(2,1)S(1)}, u32[]{:S(2)}, u32[]{:S(2)}) collective-permute-start(bf16[64,640]{1,0:T(8,128)(2,1)S(1)} %get-tuple-element.65), channel_id=1, source_target_pairs={{0,3},{1,2},{2,5},{3,4},{4,7},{5,6},{6,9},{7,8},{8,11},{9,10},{10,... | collective-permute-start | bytes 245768 | tf_op jit(solution)/shard_map/ppermute | solution.py:523
  27.4 0.5 collective-permute-start.8
  27.9 2.5 %collective-permute-start.5 = (bf16[64,640]{1,0:T(8,128)(2,1)S(1)}, bf16[64,640]{1,0:T(8,128)(2,1)S(1)}, u32[]{:S(2)}, u32[]{:S(2)}) collective-permute-start(bf16[64,640]{1,0:T(8,128)(2,1)S(1)} %get-tuple-element.67), channel_id=1, source_target_pairs={{0,30},{1,31},{2,28},{3,29},{4,26},{5,27},{6,24},{7,25},{8,22},{9,... | collective-permute-start | bytes 245768 | tf_op jit(solution)/shard_map/ppermute | solution.py:523
  30.4 2.9 %collective-permute-start.6 = (bf16[64,640]{1,0:T(8,128)(2,1)S(1)}, bf16[64,640]{1,0:T(8,128)(2,1)S(1)}, u32[]{:S(2)}, u32[]{:S(2)}) collective-permute-start(bf16[64,640]{1,0:T(8,128)(2,1)S(1)} %get-tuple-element.68), channel_id=1, source_target_pairs={{0,31},{1,30},{2,29},{3,28},{4,27},{5,26},{6,25},{7,24},{8,23},{9,... | collective-permute-start | bytes 245768 | tf_op jit(solution)/shard_map/ppermute | solution.py:523
  33.3 0.0 collective-permute-done.3.refs_0_
  33.3 2.0 %later_forward.1 = (f32[256,160]{1,0:T(8,128)S(1)}, bf16[256,160]{1,0:T(8,128)(2,1)S(1)}, bf16[256,160]{1,0:T(8,128)(2,1)S(1)}, bf16[64,640]{1,0:T(8,128)(2,1)S(1)}) custom-call(s32[2,16]{1,0:T(2,128)S(1)} %bitcast.40, bf16[64,640]{1,0:T(8,128)(2,1)S(1)} %collective-permute-done.3.refs_0_, bf16[64,640]{1,0:T(8,128)(2,1)S(1)} %collective-permute-done.4.refs_1_, ...), custom_call_target="tpu_custom_call" | custom-call | flops 235929600 | bytes 1740800 | tf_op jit(solution)/shard_map/later_forward/pallas_call | solution.py:170
  35.3 0.6 collective-permute-start.11
  35.9 1.6 %second_backward.1 = (bf16[64,640]{1,0:T(8,128)(2,1)S(1)}, bf16[256,320]{1,0:T(8,128)(2,1)S(1)}, bf16[256,160]{1,0:T(8,128)(2,1)S(1)}) custom-call(bf16[256,160]{1,0:T(8,128)(2,1)S(1)} %get-tuple-element.61.refs_5_.refs_0_, bf16[64,640]{1,0:T(8,128)(2,1)S(1)} %collective-permute-done.8.refs_1_, bf16[256,320]{1,0:T(8,128)(2,1)S(1)} %get-tuple-element.72.refs_2_.grads2, ...), custom_call_target="tpu_custom_call" | custom-call | flops 235929600 | bytes 1904640 | tf_op jit(solution)/shard_map/second_backward/pallas_call | solution.py:170
  37.5 0.0 slice-start.1
  37.5 3.2 %collective-permute-start.10 = (bf16[64,640]{1,0:T(8,128)(2,1)S(1)}, bf16[64,640]{1,0:T(8,128)(2,1)S(1)}, u32[]{:S(2)}, u32[]{:S(2)}) collective-permute-start(bf16[64,640]{1,0:T(8,128)(2,1)S(1)} %get-tuple-element.73), channel_id=1, source_target_pairs={{0,31},{1,30},{2,1},{3,0},{4,3},{5,2},{6,5},{7,4},{8,7},{9,6},{10,... | collective-permute-start | bytes 245768 | tf_op jit(solution)/shard_map/ppermute | solution.py:523
  40.7 1.3 %collective-permute-start.9 = (bf16[64,640]{1,0:T(8,128)(2,1)S(1)}, bf16[64,640]{1,0:T(8,128)(2,1)S(1)}, u32[]{:S(2)}, u32[]{:S(2)}) collective-permute-start(bf16[64,640]{1,0:T(8,128)(2,1)S(1)} %get-tuple-element.73), channel_id=1, source_target_pairs={{0,30},{1,31},{2,0},{3,1},{4,2},{5,3},{6,4},{7,5},{8,6},{9,7},{10,... | collective-permute-start | bytes 245768 | tf_op jit(solution)/shard_map/ppermute | solution.py:523
  42.1 0.2 pack_rows.1
  42.3 0.4 collective-permute-start.7
  42.6 2.0 %last_forward.1 = (bf16[128,480]{1,0:T(8,128)(2,1)S(1)}, bf16[128,480]{1,0:T(8,128)(2,1)S(1)}) custom-call(s32[2,16]{1,0:T(2,128)S(1)} %bitcast.41, f32[256,160]{1,0:T(8,128)S(1)} %get-tuple-element.76.refs_0_, bf16[64,640]{1,0:T(8,128)(2,1)S(1)} %collective-permute-done.11.refs_1_, bf16[256,160]{1,0:T(8,128)(2,1)S(1)} %get-tuple-element.78.refs_2_, ...), custom_call_target="tpu_custom_call" | custom-call | flops 235929600 | bytes 1986560 | tf_op jit(solution)/shard_map/last_forward/pallas_call | solution.py:170
  44.7 1.8 %collective-permute-start.12 = (bf16[128,480]{1,0:T(8,128)(2,1)S(1)}, bf16[128,480]{1,0:T(8,128)(2,1)S(1)}, u32[]{:S(2)}, u32[]{:S(2)}) collective-permute-start(bf16[128,480]{1,0:T(8,128)(2,1)S(1)} %get-tuple-element.81), channel_id=1, source_target_pairs={{0,1},{1,0},{2,3},{3,2},{4,5},{5,4},{6,7},{7,6},{8,9},{9,8},{10,11... | collective-permute-start | bytes 368648 | tf_op jit(solution)/shard_map/ppermute | solution.py:523
  46.5 2.4 %later_backward.1 = (bf16[256,160]{1,0:T(8,128)(2,1)S(1)}, bf16[64,640]{1,0:T(8,128)(2,1)S(1)}, bf16[256,320]{1,0:T(8,128)(2,1)S(1)}, bf16[256,160]{1,0:T(8,128)...) custom-call(s32[2,16]{1,0:T(2,128)S(1)} %bitcast.42, s32[2,16]{1,0:T(2,128)S(1)} %bitcast.47, ...), custom_call_target="tpu_custom_call" | custom-call | flops 235929600 | bytes 1986560 | tf_op jit(solution)/shard_map/later_backward/pallas_call | solution.py:170
  48.9 0.4 collective-permute-start.13
  49.3 4.3 %collective-permute-done.13.refs_1_ = bf16[64,640]{1,0:T(8,128)(2,1)S(1)} collective-permute-done((bf16[64,640]{1,0:T(8,128)(2,1)S(1)}, bf16[64,640]{1,0:T(8,128)(2,1)S(1)}, u32[]{:S(2)}, u32[]{:S(2)}) %collective-permute-start.13) | collective-permute-done | bytes 81952 | tf_op jit(solution)/shard_map/ppermute | solution.py:523
  53.6 2.3 %last_backward.1 = (bf16[32,640]{1,0:T(8,128)(2,1)S(1)}, bf16[32,640]{1,0:T(8,128)(2,1)S(1)}, bf16[128,320]{1,0:T(8,128)(2,1)S(1)}, bf16[256,320]{1,0:T(8,128)(2,1)S(1)}, bf16[256,160]{1,0:T(8,128)(2,1)S(1)}) custom-call(s32[2,16]{1,0:T(2,128)S(1)} %bitcast.43, s32[2,16]{1,0:T(2,128)S(1)} %bitcast.48, bf16[256,160]{1,0:T(8,128)(2,1)S(1)} %get-tuple-element.82.refs_0_, ...), custom_call_target="tpu_custom_call" | custom-call | flops 235929600 | bytes 1986560 | tf_op jit(solution)/shard_map/last_backward/pallas_call | solution.py:170
  55.9 2.1 %collective-permute-start.16 = (bf16[32,640]{1,0:T(8,128)(2,1)S(1)}, bf16[32,640]{1,0:T(8,128)(2,1)S(1)}, u32[]{:S(2)}, u32[]{:S(2)}) collective-permute-start(bf16[32,640]{1,0:T(8,128)(2,1)S(1)} %get-tuple-element.89), channel_id=1, source_target_pairs={{0,30},{1,31},{2,0},{3,1},{4,2},{5,3},{6,4},{7,5},{8,6},{9,7},{10,... | collective-permute-start | bytes 122888 | tf_op jit(solution)/shard_map/ppermute | solution.py:523
  58.0 0.8 %collective-permute-start.17 = (bf16[32,640]{1,0:T(8,128)(2,1)S(1)}, bf16[32,640]{1,0:T(8,128)(2,1)S(1)}, u32[]{:S(2)}, u32[]{:S(2)}) collective-permute-start(bf16[32,640]{1,0:T(8,128)(2,1)S(1)} %get-tuple-element.90), channel_id=1, source_target_pairs={{0,31},{1,30},{2,1},{3,0},{4,3},{5,2},{6,5},{7,4},{8,7},{9,6},{10,... | collective-permute-start | bytes 122888 | tf_op jit(solution)/shard_map/ppermute | solution.py:523
  58.8 0.1 add_rows.1
  58.9 1.2 %collective-permute-start.15 = (bf16[128,320]{1,0:T(8,128)(2,1)S(1)}, bf16[128,320]{1,0:T(8,128)(2,1)S(1)}, u32[]{:S(2)}, u32[]{:S(2)}) collective-permute-start(bf16[128,320]{1,0:T(8,128)(2,1)S(1)} %get-tuple-element.88), channel_id=1, source_target_pairs={{0,30},{1,31},{2,28},{3,29},{4,26},{5,27},{6,24},{7,25},{8,22},{9,... | collective-permute-start | bytes 245768 | tf_op jit(solution)/shard_map/ppermute | solution.py:523
  60.1 0.2 collective-permute-start.14
  60.3 0.0 copy-start.3
  60.3 0.0 copy-start.5
  60.3 0.0 copy-start.7
  60.3 9.5 %kernel_grads.1 = f32[18,160,320]{2,1,0:T(8,128)} custom-call(bf16[256,160]{1,0:T(8,128)(2,1)S(1)} %get-tuple-element.95.acts0, bf16[256,160]{1,0:T(8,128)(2,1)S(1)} %get-tuple-element.96.acts1, bf16[256,320]{1,0:T(8,128)(2,1)S(1)} %get-tuple-element.97.grads0, bf16[256,320]{1,0:T(8,128)(2,1)S(1)} %get-tuple-element.98.grads1, ...), custom_call_target="tpu_custom_call" | custom-call | flops 943718400 | bytes 7372800 | tf_op jit(solution)/shard_map/kernel_grads/pallas_call | solution.py:627
  69.9 2.2 %finish.1 = (bf16[3,128,320]{2,1,0:T(8,128)(2,1)}, bf16[3,128,320]{2,1,0:T(8,128)(2,1)}, bf16[3,128,320]{2,1,0:T(8,128)(2,1)}, bf16[6,128,320]{2,1,0:T(8,128)(2,1)}, bf16[2,128,320]{2,1,0:T(8,128)(2,1)}) custom-call(s32[2,16]{1,0:T(2,128)S(1)} %bitcast.44, s32[2,16]{1,0:T(2,128)S(1)} %bitcast.49, bf16[3,128,320]{2,1,0:T(8,128)(2,1)S(1)} %bitcast.31, ...), custom_call_target="tpu_custom_call" | custom-call | bytes 2375680 | tf_op jit(solution)/shard_map/finish/pallas_call | solution.py:170
  (30 shorter events, 0.1 us)
Async XLA Ops:
  0.6 1.1 %copy-start = (bf16[1,3,2,4,32,320]{5,4,3,2,1,0:T(8,128)(2,1)S(1)}, bf16[1,3,2,4,32,320]{5,4,3,2,1,0:T(8,128)(2,1)}, u32[]{:S(2)}) copy-start(bf16[1,3,2,4,32,320]{5,4,3,2,1,0:T(8,128)(2,1)} %param.11) | copy-start | bytes 1474564
  1.7 1.0 %copy-start.2 = (bf16[1,3,4,32,320]{4,3,2,1,0:T(8,128)(2,1)S(1)}, bf16[1,3,4,32,320]{4,3,2,1,0:T(8,128)(2,1)}, u32[]{:S(2)}) copy-start(bf16[1,3,4,32,320]{4,3,2,1,0:T(8,128)(2,1)} %param.8) | copy-start | bytes 737284
  2.7 1.0 %copy-start.4 = (bf16[1,3,4,32,320]{4,3,2,1,0:T(8,128)(2,1)S(1)}, bf16[1,3,4,32,320]{4,3,2,1,0:T(8,128)(2,1)}, u32[]{:S(2)}) copy-start(bf16[1,3,4,32,320]{4,3,2,1,0:T(8,128)(2,1)} %param.9) | copy-start | bytes 737284
  3.6 1.0 %copy-start.6 = (bf16[1,3,4,32,320]{4,3,2,1,0:T(8,128)(2,1)S(1)}, bf16[1,3,4,32,320]{4,3,2,1,0:T(8,128)(2,1)}, u32[]{:S(2)}) copy-start(bf16[1,3,4,32,320]{4,3,2,1,0:T(8,128)(2,1)} %param.10) | copy-start | bytes 737284
  4.6 0.7 copy-start.8
  5.3 0.7 copy-start.9
  5.9 4.9 %copy-start.10 = (bf16[1,2,3,3,160,320]{5,4,3,2,1,0:T(8,128)(2,1)S(1)}, bf16[1,2,3,3,160,320]{5,4,3,2,1,0:T(8,128)(2,1)}, u32[]{:S(2)}) copy-start(bf16[1,2,3,3,160,320]{5,4,3,2,1,0:T(8,128)(2,1)} %param.12) | copy-start | bytes 5529604
  6.7 8.1 %collective-permute-start = (bf16[128,640]{1,0:T(8,128)(2,1)S(1)}, bf16[128,640]{1,0:T(8,128)(2,1)S(1)}, u32[]{:S(2)}, u32[]{:S(2)}) collective-permute-start(bf16[128,640]{1,0:T(8,128)(2,1)S(1)} %get-tuple-element.55), channel_id=1, source_target_pairs={{0,1},{1,0},{2,3},{3,2},{4,5},{5,4},{6,7},{7,6},{8,9},{9,8},{10,11... | collective-permute-start | bytes 491528 | tf_op jit(solution)/shard_map/ppermute | solution.py:523
  10.8 11.9 %collective-permute-start.2 = (bf16[128,1280]{1,0:T(8,128)(2,1)S(1)}, bf16[128,1280]{1,0:T(8,128)(2,1)S(1)}, u32[]{:S(2)}, u32[]{:S(2)}) collective-permute-start(bf16[128,1280]{1,0:T(8,128)(2,1)S(1)} %get-tuple-element.60), channel_id=1, source_target_pairs={{0,1},{1,0},{2,3},{3,2},{4,5},{5,4},{6,7},{7,6},{8,9},{9,8},{10,11... | collective-permute-start | bytes 983048 | tf_op jit(solution)/shard_map/ppermute | solution.py:523
  16.2 6.6 %collective-permute-start.1 = (bf16[64,640]{1,0:T(8,128)(2,1)S(1)}, bf16[64,640]{1,0:T(8,128)(2,1)S(1)}, u32[]{:S(2)}, u32[]{:S(2)}) collective-permute-start(bf16[64,640]{1,0:T(8,128)(2,1)S(1)} %get-tuple-element.57), channel_id=1, source_target_pairs={{0,1},{1,0},{2,3},{3,2},{4,5},{5,4},{6,7},{7,6},{8,9},{9,8},{10,11... | collective-permute-start | bytes 245768 | tf_op jit(solution)/shard_map/ppermute | solution.py:523
  18.3 42.0 %slice-start = ((s8[4423680]{0:T(1024)(128)(4,1)}), s8[4194304]{0:T(1024)(128)(4,1)S(1)}, s32[]{:S(2)}) async-start(s8[4423680]{0:T(1024)(128)(4,1)} %bitcast.26), calls=%async_computation | async-start | bytes 8388608
  24.4 8.9 %collective-permute-start.3 = (bf16[64,640]{1,0:T(8,128)(2,1)S(1)}, bf16[64,640]{1,0:T(8,128)(2,1)S(1)}, u32[]{:S(2)}, u32[]{:S(2)}) collective-permute-start(bf16[64,640]{1,0:T(8,128)(2,1)S(1)} %get-tuple-element.64), channel_id=1, source_target_pairs={{0,2},{1,3},{2,4},{3,5},{4,6},{5,7},{6,8},{7,9},{8,10},{9,11},{10,... | collective-permute-start | bytes 245768 | tf_op jit(solution)/shard_map/ppermute | solution.py:523
  24.4 8.9 %collective-permute-start.4 = (bf16[64,640]{1,0:T(8,128)(2,1)S(1)}, bf16[64,640]{1,0:T(8,128)(2,1)S(1)}, u32[]{:S(2)}, u32[]{:S(2)}) collective-permute-start(bf16[64,640]{1,0:T(8,128)(2,1)S(1)} %get-tuple-element.65), channel_id=1, source_target_pairs={{0,3},{1,2},{2,5},{3,4},{4,7},{5,6},{6,9},{7,8},{8,11},{9,10},{10,... | collective-permute-start | bytes 245768 | tf_op jit(solution)/shard_map/ppermute | solution.py:523
  27.4 8.5 %collective-permute-start.8 = (bf16[64,640]{1,0:T(8,128)(2,1)S(1)}, bf16[64,640]{1,0:T(8,128)(2,1)S(1)}, u32[]{:S(2)}, u32[]{:S(2)}) collective-permute-start(bf16[64,640]{1,0:T(8,128)(2,1)S(1)} %get-tuple-element.71), channel_id=1, source_target_pairs={{0,1},{1,0},{2,3},{3,2},{4,5},{5,4},{6,7},{7,6},{8,9},{9,8},{10,11... | collective-permute-start | bytes 245768 | tf_op jit(solution)/shard_map/ppermute | solution.py:523
  27.9 14.2 %collective-permute-start.5 = (bf16[64,640]{1,0:T(8,128)(2,1)S(1)}, bf16[64,640]{1,0:T(8,128)(2,1)S(1)}, u32[]{:S(2)}, u32[]{:S(2)}) collective-permute-start(bf16[64,640]{1,0:T(8,128)(2,1)S(1)} %get-tuple-element.67), channel_id=1, source_target_pairs={{0,30},{1,31},{2,28},{3,29},{4,26},{5,27},{6,24},{7,25},{8,22},{9,... | collective-permute-start | bytes 245768 | tf_op jit(solution)/shard_map/ppermute | solution.py:523
  30.4 11.7 %collective-permute-start.6 = (bf16[64,640]{1,0:T(8,128)(2,1)S(1)}, bf16[64,640]{1,0:T(8,128)(2,1)S(1)}, u32[]{:S(2)}, u32[]{:S(2)}) collective-permute-start(bf16[64,640]{1,0:T(8,128)(2,1)S(1)} %get-tuple-element.68), channel_id=1, source_target_pairs={{0,31},{1,30},{2,29},{3,28},{4,27},{5,26},{6,25},{7,24},{8,23},{9,... | collective-permute-start | bytes 245768 | tf_op jit(solution)/shard_map/ppermute | solution.py:523
  35.3 7.3 %collective-permute-start.11 = (bf16[64,640]{1,0:T(8,128)(2,1)S(1)}, bf16[64,640]{1,0:T(8,128)(2,1)S(1)}, u32[]{:S(2)}, u32[]{:S(2)}) collective-permute-start(bf16[64,640]{1,0:T(8,128)(2,1)S(1)} %get-tuple-element.77), channel_id=1, source_target_pairs={{0,1},{1,0},{2,3},{3,2},{4,5},{5,4},{6,7},{7,6},{8,9},{9,8},{10,11... | collective-permute-start | bytes 245768 | tf_op jit(solution)/shard_map/ppermute | solution.py:523
  37.5 22.8 %slice-start.1 = ((s8[4423680]{0:T(1024)(128)(4,1)}), s8[229376]{0:T(1024)(128)(4,1)S(1)}, s32[]{:S(2)}) async-start(s8[4423680]{0:T(1024)(128)(4,1)} %bitcast.26), calls=%async_computation.1 | async-start | bytes 458752
  37.5 9.0 %collective-permute-start.10 = (bf16[64,640]{1,0:T(8,128)(2,1)S(1)}, bf16[64,640]{1,0:T(8,128)(2,1)S(1)}, u32[]{:S(2)}, u32[]{:S(2)}) collective-permute-start(bf16[64,640]{1,0:T(8,128)(2,1)S(1)} %get-tuple-element.73), channel_id=1, source_target_pairs={{0,31},{1,30},{2,1},{3,0},{4,3},{5,2},{6,5},{7,4},{8,7},{9,6},{10,... | collective-permute-start | bytes 245768 | tf_op jit(solution)/shard_map/ppermute | solution.py:523
  40.7 5.8 %collective-permute-start.9 = (bf16[64,640]{1,0:T(8,128)(2,1)S(1)}, bf16[64,640]{1,0:T(8,128)(2,1)S(1)}, u32[]{:S(2)}, u32[]{:S(2)}) collective-permute-start(bf16[64,640]{1,0:T(8,128)(2,1)S(1)} %get-tuple-element.73), channel_id=1, source_target_pairs={{0,30},{1,31},{2,0},{3,1},{4,2},{5,3},{6,4},{7,5},{8,6},{9,7},{10,... | collective-permute-start | bytes 245768 | tf_op jit(solution)/shard_map/ppermute | solution.py:523
  42.3 27.6 %collective-permute-start.7 = (bf16[128,800]{1,0:T(8,128)(2,1)S(1)}, bf16[128,800]{1,0:T(8,128)(2,1)S(1)}, u32[]{:S(2)}, u32[]{:S(2)}) collective-permute-start(bf16[128,800]{1,0:T(8,128)(2,1)S(1)} %get-tuple-element.70), channel_id=1, source_target_pairs={{0,1},{1,0},{2,3},{3,2},{4,5},{5,4},{6,7},{7,6},{8,9},{9,8},{10,11... | collective-permute-start | bytes 614408 | tf_op jit(solution)/shard_map/ppermute | solution.py:523
  44.7 14.1 %collective-permute-start.12 = (bf16[128,480]{1,0:T(8,128)(2,1)S(1)}, bf16[128,480]{1,0:T(8,128)(2,1)S(1)}, u32[]{:S(2)}, u32[]{:S(2)}) collective-permute-start(bf16[128,480]{1,0:T(8,128)(2,1)S(1)} %get-tuple-element.81), channel_id=1, source_target_pairs={{0,1},{1,0},{2,3},{3,2},{4,5},{5,4},{6,7},{7,6},{8,9},{9,8},{10,11... | collective-permute-start | bytes 368648 | tf_op jit(solution)/shard_map/ppermute | solution.py:523
  48.9 4.7 %collective-permute-start.13 = (bf16[64,640]{1,0:T(8,128)(2,1)S(1)}, bf16[64,640]{1,0:T(8,128)(2,1)S(1)}, u32[]{:S(2)}, u32[]{:S(2)}) collective-permute-start(bf16[64,640]{1,0:T(8,128)(2,1)S(1)} %get-tuple-element.83), channel_id=1, source_target_pairs={{0,1},{1,0},{2,3},{3,2},{4,5},{5,4},{6,7},{7,6},{8,9},{9,8},{10,11... | collective-permute-start | bytes 245768 | tf_op jit(solution)/shard_map/ppermute | solution.py:523
  55.9 14.0 %collective-permute-start.16 = (bf16[32,640]{1,0:T(8,128)(2,1)S(1)}, bf16[32,640]{1,0:T(8,128)(2,1)S(1)}, u32[]{:S(2)}, u32[]{:S(2)}) collective-permute-start(bf16[32,640]{1,0:T(8,128)(2,1)S(1)} %get-tuple-element.89), channel_id=1, source_target_pairs={{0,30},{1,31},{2,0},{3,1},{4,2},{5,3},{6,4},{7,5},{8,6},{9,7},{10,... | collective-permute-start | bytes 122888 | tf_op jit(solution)/shard_map/ppermute | solution.py:523
  58.0 11.9 %collective-permute-start.17 = (bf16[32,640]{1,0:T(8,128)(2,1)S(1)}, bf16[32,640]{1,0:T(8,128)(2,1)S(1)}, u32[]{:S(2)}, u32[]{:S(2)}) collective-permute-start(bf16[32,640]{1,0:T(8,128)(2,1)S(1)} %get-tuple-element.90), channel_id=1, source_target_pairs={{0,31},{1,30},{2,1},{3,0},{4,3},{5,2},{6,5},{7,4},{8,7},{9,6},{10,... | collective-permute-start | bytes 122888 | tf_op jit(solution)/shard_map/ppermute | solution.py:523
  58.9 11.0 %collective-permute-start.15 = (bf16[128,320]{1,0:T(8,128)(2,1)S(1)}, bf16[128,320]{1,0:T(8,128)(2,1)S(1)}, u32[]{:S(2)}, u32[]{:S(2)}) collective-permute-start(bf16[128,320]{1,0:T(8,128)(2,1)S(1)} %get-tuple-element.88), channel_id=1, source_target_pairs={{0,30},{1,31},{2,28},{3,29},{4,26},{5,27},{6,24},{7,25},{8,22},{9,... | collective-permute-start | bytes 245768 | tf_op jit(solution)/shard_map/ppermute | solution.py:523
  60.1 9.8 %collective-permute-start.14 = (bf16[128,320]{1,0:T(8,128)(2,1)S(1)}, bf16[128,320]{1,0:T(8,128)(2,1)S(1)}, u32[]{:S(2)}, u32[]{:S(2)}) collective-permute-start(bf16[128,320]{1,0:T(8,128)(2,1)S(1)} %get-tuple-element.86.refs_8_), channel_id=1, source_target_pairs={{0,2},{1,3},{2,4},{3,5},{4,6},{5,7},{6,8},{7,9},{8,10},{9,11},{10,... | collective-permute-start | bytes 245768 | tf_op jit(solution)/shard_map/ppermute | solution.py:523
  60.3 9.6 %copy-start.1 = (bf16[1,3,2,4,32,320]{5,4,3,2,1,0:T(8,128)(2,1)S(1)}, bf16[1,3,2,4,32,320]{5,4,3,2,1,0:T(8,128)(2,1)}, u32[]{:S(2)}) copy-start(bf16[1,3,2,4,32,320]{5,4,3,2,1,0:T(8,128)(2,1)} %param.11) | copy-start | bytes 1474564
  60.3 9.6 %copy-start.3 = (bf16[1,3,4,32,320]{4,3,2,1,0:T(8,128)(2,1)S(1)}, bf16[1,3,4,32,320]{4,3,2,1,0:T(8,128)(2,1)}, u32[]{:S(2)}) copy-start(bf16[1,3,4,32,320]{4,3,2,1,0:T(8,128)(2,1)} %param.8) | copy-start | bytes 737284
  60.3 9.6 %copy-start.5 = (bf16[1,3,4,32,320]{4,3,2,1,0:T(8,128)(2,1)S(1)}, bf16[1,3,4,32,320]{4,3,2,1,0:T(8,128)(2,1)}, u32[]{:S(2)}) copy-start(bf16[1,3,4,32,320]{4,3,2,1,0:T(8,128)(2,1)} %param.9) | copy-start | bytes 737284
  60.3 9.6 %copy-start.7 = (bf16[1,3,4,32,320]{4,3,2,1,0:T(8,128)(2,1)S(1)}, bf16[1,3,4,32,320]{4,3,2,1,0:T(8,128)(2,1)}, u32[]{:S(2)}) copy-start(bf16[1,3,4,32,320]{4,3,2,1,0:T(8,128)(2,1)} %param.10) | copy-start | bytes 737284
